TPU v7x, 32 devices: a whole 2x2x4 slice. The times are simulated.
32 devices in a mesh: mapx: 8 (over z, x), mapy: 2 (over y), layer: 2 (over core).
Axes of the slice: x: 2, y: 2, z: 4, core: 2. Of those that a mesh axis runs over, the one named last changes fastest.
Arguments:
- old_state: float32 [8, 2, 2, 6, 8192], P('mapx', 'mapy', 'layer'), as said below
- send_blocks: int32 [8, 2, 2, 10, 16], P('mapx', 'mapy', 'layer'), may hold values from 0 to 63
- node_slots: int32 [8, 2, 2, 4, 512], P('mapx', 'mapy', 'layer'), may hold values from 0 to 20479, as said below
- node_weights: float32 [8, 2, 2, 4, 512], P('mapx', 'mapy', 'layer'), as said below
- front_mask: int32 [8, 2, 2, 512], P('mapx', 'mapy', 'layer'), may hold values 0 or 1
- halo_lists: int32 [8, 2, 2, 6, 256], P('mapx', 'mapy', 'layer'), may hold values from 0 to 511
- elem_nodes: int32 [8, 2, 2, 4, 2560], P('mapx', 'mapy', 'layer'), may hold values from 0 to 2047
- shape_grads: float32 [8, 2, 2, 12, 2560], P('mapx', 'mapy', 'layer'), as said below
- elem_volume: float32 [8, 2, 2, 2560], P('mapx', 'mapy', 'layer'), may hold values from 0.5 to 2
Outputs:
- new_state: float32 [8, 2, 2, 6, 512], P('mapx', 'mapy', 'layer')
- residual: float32 [8, 2, 2, 4, 512], P('mapx', 'mapy', 'layer')
Inputs may be any that keep to these rules, and one draw needn't show every extreme that they name: `send_blocks`: each entry names one of the sender's old blocks; a block may go to several peers or twice to one. `node_slots`: indexes the received nodes, ordered by source (mapx offset plus 2, times 2, plus layer index), then slot, then node in the block; only sources inside the device grid are named. `node_weights`: Positive; the four weights of a node sum to one. `halo_lists`: owned nodes kept as ghosts by the neighbour in direction k. `elem_nodes`: local numbering: the owned nodes first, then 256 ghosts for each of the six directions in order. `shape_grads`: the four gradients of an element sum to zero. `old_state`: rows 0 to 3 velocity and pressure, row 4 temperature in [-1, 0], row 5 damage in [0, 0.9].
All inputs are finite; a program needn't handle non-finite values. No bound on the sum of `front_mask` on one device may be relied on, other than what follows from the above.
Results may differ from a plain program's by a relative error of at most 0.00002.
Values sent between devices are 32-bit elements; how exact they have to be, the bound alone decides.
No kernel may reach another device: no remote copies, remote signals or barrier semaphores. Data moves between devices by JAX's collectives and lax.ppermute only.
A program may use at most 64 MiB of HBM per device.

v0:
```python
import functools

import jax
import jax.numpy as jnp
from jax import lax
from jax.experimental import pallas as pl
from jax.experimental.pallas import tpu as pltpu
from jax.sharding import PartitionSpec as P

BLOCK = 128
REACH = 2
FIELDS = 6
SPLITS = 3

ocean_temp = 0.0
strain_reg = 0.01
gravity = 0.5

AXES = ("mapx", "mapy", "layer")
VMEM = pl.BlockSpec(memory_space=pltpu.VMEM)
SMEM = pl.BlockSpec(memory_space=pltpu.SMEM)


def params():
    return pltpu.CompilerParams(vmem_limit_bytes=32 * 1024 * 1024)


def both_ways(pairs):
    return [way for one, other in pairs for way in ((one, other), (other, one))]


def column_moves(count):
    outside = [(at, at + 1) for at in range(1, count - 1, 2)]
    inside = [(at, at + 1) for at in range(0, count - 1, 2)]
    within = [(at + i, at + i + 2) for at in range(0, count - 3, 4) for i in range(2)]
    across = [(at + i, at + i + 2) for at in range(2, count - 3, 4) for i in range(2)]
    number = lambda pairs, layer: [(one * 2 + layer, other * 2 + layer) for one, other in pairs]
    return [
        both_ways(number(outside, 1) + number(inside, 0)),
        both_ways(number(within, 0) + number(across, 1)),
    ]


def column_offsets(layer):
    at = lax.axis_index("mapx")
    near = jnp.where(lax.rem(at, 2) == 0, 1, -1)
    two = jnp.where(lax.rem(at, 4) < 2, 2, -2)
    return [jnp.where(layer == 0, near, -near), jnp.where(layer == 0, two, -two)]


def pair_swap(value, axis, count, first):
    return lax.ppermute(value, axis, both_ways([(at, at + 1) for at in range(first, count - 1, 2)]))


def swap_all(values, sizes):
    long = [axis for axis in range(3) if sizes[axis] > 2]
    steps = [(axis, 1) for axis in long] + [(axis, 0) for axis in range(3)]
    return [pair_swap(value, AXES[axis], sizes[axis], first) for value, (axis, first) in zip(values, steps)]


def pack_blocks(blocks_ref, old_ref, ref, offset):
    slots = blocks_ref.shape[2]
    stride = old_ref.shape[0] // FIELDS
    for to_layer in range(2):
        peer = (offset + REACH) * 2 + to_layer
        start = to_layer * FIELDS * slots
        for c in range(slots):
            rows = pl.ds(blocks_ref[peer, 0, c], FIELDS, stride=stride)
            ref[start + FIELDS * c : start + FIELDS * (c + 1), :] = old_ref[rows, :]


def give_kernel(count, *refs):
    blocks_in_ref, old_in_ref = refs[:2]
    give_first_ref, give_ref, old_ref = refs[2 + count : 5 + count]
    held = refs[5 + count : 5 + 2 * count]
    blocks_ref, sems = refs[5 + 2 * count :]
    first = [pltpu.make_async_copy(blocks_in_ref, blocks_ref, sems.at[0])]
    first += [pltpu.make_async_copy(old_in_ref, old_ref, sems.at[1])]
    rest = [pltpu.make_async_copy(refs[2 + i], held[i], sems.at[2 + i]) for i in range(count)]
    for copy in first + rest:
        copy.start()
    for copy in first:
        copy.wait()
    offsets = column_offsets(1 - lax.axis_index("layer"))
    pack_blocks(blocks_ref, old_ref, give_first_ref, offsets[0])
    pack_blocks(blocks_ref, old_ref, give_ref, offsets[1])
    for copy in rest:
        copy.wait()
    size = give_first_ref.shape[0]
    slots_ref, weights_ref = held[0], held[1]
    slot_rows = slots_ref.shape[0] * slots_ref.shape[1] // BLOCK
    cut_rows(slots_ref, give_ref.at[size : size + slot_rows])
    cut_rows(weights_ref, give_ref.at[size + slot_rows : size + 2 * slot_rows])


def keep_kernel(blocks_ref, old_ref, first_ref, second_ref):
    offsets = column_offsets(lax.axis_index("layer"))
    pack_blocks(blocks_ref, old_ref, first_ref, offsets[0])
    pack_blocks(blocks_ref, old_ref, second_ref, offsets[1])


def pick(row, lanes):
    return jnp.take_along_axis(jnp.broadcast_to(row, lanes.shape), lanes, axis=1)


def pick_fields(table_ref, block_count, blocks, lanes):
    found = [jnp.zeros((8, BLOCK), jnp.float32) for _ in range(FIELDS)]
    for b in range(block_count):
        hit = blocks == b
        for f in range(FIELDS):
            row = table_ref[b // 2, 2 * f + b % 2 : 2 * f + b % 2 + 1, :]
            found[f] = jnp.where(hit, pick(row, lanes), found[f])
    return found


def add_blocks(ref, chunk, first_block, blocks, lanes, found):
    local = blocks - first_block
    found = list(found)
    for c in range(ref.shape[1] // FIELDS):
        hit = local == c
        for f in range(FIELDS):
            row = ref[chunk, FIELDS * c + f : FIELDS * c + f + 1, :]
            found[f] = jnp.where(hit, pick(row, lanes), found[f])
    return tuple(found)


def add_chunks(ref, numbers, offset, ids, found):
    blocks, lanes = ids >> 7, ids & (BLOCK - 1)
    for chunk, layer in numbers:
        first = ((offset + REACH) * 2 + layer) * (ref.shape[1] // FIELDS)
        found = add_blocks(ref, chunk, first, blocks, lanes, found)
    return found


def load_fields(found_ref, owner, v):
    return tuple(found_ref[owner, f, 8 * v : 8 * v + 8, :] for f in range(FIELDS))


def save_fields(found_ref, owner, v, found):
    for f in range(FIELDS):
        found_ref[owner, f, 8 * v : 8 * v + 8, :] = found[f]


def arrived_chunks(ref, move, ids, found, owner):
    layer = lax.axis_index("layer")
    to_layer = 1 - layer if owner else layer
    numbers = [(to_layer, layer), (2 + to_layer, 1 - layer)]
    return add_chunks(ref, numbers, column_offsets(layer)[move], ids, found)


def cut_rows(from_ref, to_ref):
    count = from_ref.shape[1] // BLOCK
    for r in range(from_ref.shape[0]):
        for i in range(count):
            to_ref[r * count + i : r * count + i + 1, :] = from_ref[
                r : r + 1, i * BLOCK : (i + 1) * BLOCK
            ].astype(to_ref.dtype)


def lane_one_hot(ids):
    rows = lax.broadcasted_iota(jnp.int32, (BLOCK, BLOCK), 0)
    hit = rows == jnp.broadcast_to(ids & (BLOCK - 1), rows.shape)
    return jnp.where(hit, 1.0, 0.0).T.astype(jnp.bfloat16)


def own_kernel(
    blocks_ref,
    old_ref,
    other_slots_ref,
    slots_in_ref,
    weights_in_ref,
    halos_in_ref,
    nodes_in_ref,
    volume_in_ref,
    found_ref,
    slots_ref,
    weights_ref,
    halos_ref,
    nodes_ref,
    volume_ref,
    halo_hot_ref,
    node_hot_ref,
    own_ref,
):
    for layer in range(2):
        chunk_ref = own_ref.at[layer]
        for c in range(blocks_ref.shape[2]):
            rows = pl.ds(blocks_ref[2 * REACH + layer, 0, c], FIELDS, stride=old_ref.shape[0] // FIELDS)
            chunk_ref[FIELDS * c : FIELDS * (c + 1), :] = old_ref[rows, :]
    for k in range(halos_in_ref.shape[0]):
        cut_rows(halos_in_ref.at[k], halos_ref.at[2 * k : 2 * k + 2])
    cut_rows(slots_in_ref, slots_ref.at[0])
    slots_ref[1] = other_slots_ref[...].astype(jnp.int32)
    cut_rows(weights_in_ref, weights_ref)
    cut_rows(nodes_in_ref, nodes_ref)
    cut_rows(volume_in_ref, volume_ref)
    layer = lax.axis_index("layer")
    for owner in range(2):
        for v in range(slots_ref.shape[1] // 8):
            ids = slots_ref[owner, 8 * v : 8 * v + 8, :]
            found = tuple(jnp.zeros((8, BLOCK), jnp.float32) for _ in range(FIELDS))
            numbers = [(1 - layer if owner else layer, layer)]
            save_fields(found_ref, owner, v, add_chunks(own_ref, numbers, 0, ids, found))
    for r in range(halos_ref.shape[0]):
        halo_hot_ref[r * BLOCK : (r + 1) * BLOCK, :] = lane_one_hot(halos_ref[r : r + 1, :])
    steps, width, _ = node_hot_ref.shape
    group = width // BLOCK

    def hot(step, carry):
        for r in range(group):
            ids = nodes_ref[pl.ds(step * group + r, 1), :]
            node_hot_ref[step, r * BLOCK : (r + 1) * BLOCK, :] = lane_one_hot(ids)
        return carry

    lax.fori_loop(0, steps, hot, 0)


def early_kernel(came_ref, slots_ref, found_in_ref, found_ref):
    for owner in range(2):
        for v in range(slots_ref.shape[1] // 8):
            ids = slots_ref[owner, 8 * v : 8 * v + 8, :]
            found = arrived_chunks(came_ref, 0, ids, load_fields(found_in_ref, owner, v), owner)
            save_fields(found_ref, owner, v, found)


def late_kernel(rows, came_ref, slots_ref, found_ref, weights_ref, other_weights_ref, mine_ref, other_ref):
    for owner, out_ref, weight_ref in ((1, other_ref, other_weights_ref), (0, mine_ref, weights_ref)):
        totals = [jnp.zeros((rows, BLOCK), jnp.float32) for _ in range(FIELDS)]
        for v in range(slots_ref.shape[1] // 8):
            ids = slots_ref[owner, 8 * v : 8 * v + 8, :]
            found = arrived_chunks(came_ref, 1, ids, load_fields(found_ref, owner, v), owner)
            for f in range(FIELDS):
                term = found[f] * weight_ref[8 * v : 8 * v + 8, :]
                for k in range(8 // rows):
                    totals[f] = totals[f] + term[k * rows : (k + 1) * rows, :]
        for f in range(FIELDS):
            out_ref[f * rows : (f + 1) * rows, :] = totals[f]


def state_kernel(counts, mine_ref, came_ref, mask_ref, halos_ref, state_ref, table_ref, *more_refs):
    send_refs, cut_ref = more_refs[:-1], more_refs[-1]
    front = mask_ref[...] == 1
    rows = mask_ref.shape[0]
    for f in range(FIELDS):
        at = slice(f * rows, (f + 1) * rows)
        total = mine_ref[at, :] + came_ref[at, :]
        if f == 4:
            total = jnp.where(front, ocean_temp, total)
        state_ref[f * rows : (f + 1) * rows, :] = total
        for s in range(rows // 2):
            table_ref[s, 2 * f : 2 * f + 2, :] = total[2 * s : 2 * s + 2, :]
    starts = (0, halos_ref.shape[0] - 8)
    halo = [halos_ref[first : first + 8, :] for first in starts]
    halo_blocks = [i >> 7 for i in halo]
    halo_lanes = [i & (BLOCK - 1) for i in halo]
    for v in range(2):
        cut = pick_fields(table_ref, rows, halo_blocks[v], halo_lanes[v])
        for k in range(6):
            r = 2 * k - starts[v]
            if 0 <= r <= 6:
                for f in range(FIELDS):
                    cut_ref[k, 2 * f : 2 * f + 2, :] = cut[f][r : r + 2, :]
    send_pairs(counts, cut_ref, send_refs, [(0, 1), (2, 3), (4, 5)])


def pair_places():
    return [lax.rem(lax.axis_index(axis), 2) for axis in AXES]


def send_pairs(counts, cut_ref, send_refs, order):
    places = pair_places()
    long = [axis for axis in range(3) if counts[axis] > 2]
    for axis in range(3):
        even, odd = order[axis]
        send_refs[len(long) + axis][...] = cut_ref[jnp.where(places[axis] == 0, even, odd)]
        if axis in long:
            send_refs[long.index(axis)][...] = cut_ref[jnp.where(places[axis] == 0, odd, even)]


def placed(values, ids, block_count):
    rows = lax.broadcasted_iota(jnp.int32, (block_count, BLOCK), 0)
    hit = rows == jnp.broadcast_to(ids >> 7, rows.shape)
    left = [jnp.where(hit, jnp.broadcast_to(v, rows.shape), 0.0) for v in values]
    return jnp.concatenate(left, axis=0).astype(jnp.bfloat16)


def cut_parts(value):
    parts = []
    for _ in range(SPLITS - 1):
        part = value.astype(jnp.bfloat16).astype(jnp.float32)
        parts.append(part)
        value = value - part
    return parts + [value]


def hot_dot(left, right):
    return jnp.dot(left, right, preferred_element_type=jnp.float32)


def came_slots(counts):
    places = pair_places()
    long = [axis for axis in range(3) if counts[axis] > 2]
    slots = []
    for axis in long:
        at = lax.axis_index(AXES[axis])
        edge = jnp.where(places[axis] == 0, at == 0, at == counts[axis] - 1)
        slots.append(jnp.where(edge, -(1 << 10), 2 * axis + places[axis]))
    return slots + [2 * axis + 1 - places[axis] for axis in range(3)]


def moved_axes(counts):
    return [axis for axis in range(3) if counts[axis] > 2] + [0, 1, 2]


def add_slot(read, slot, ids, found):
    blocks, lanes = (ids >> 7) - 2 * slot, ids & (BLOCK - 1)
    found = list(found)
    for h in range(2):
        hit = blocks == h
        for f in range(FIELDS):
            found[f] = jnp.where(hit, pick(read(2 * f + h), lanes), found[f])
    return found


def values_kernel(counts, table_ref, nodes_ref, *refs):
    came_refs, values_ref = refs[:-1], refs[-1]
    owned_slots = table_ref.shape[0]
    slots = [slot for slot, axis in zip(came_slots(counts), moved_axes(counts)) if axis == 0]
    for first in range(0, nodes_ref.shape[0], 8):
        ids = nodes_ref[first : first + 8, :]
        found = [jnp.zeros((8, BLOCK), jnp.float32) for _ in range(FIELDS)]
        for s in range(owned_slots):
            found = add_slot(lambda r: table_ref[s, r : r + 1, :], s, ids, found)
        for ref, slot in zip(came_refs, slots):
            found = add_slot(lambda r: ref[r : r + 1, :], owned_slots + slot, ids, found)
        for f in range(FIELDS):
            values_ref[f, first : first + 8, :] = found[f]


def element_kernel(counts, moves, owned_slots, *refs):
    values_in_ref, nodes_ref, node_hot_ref, grads_ref, volume_ref = refs[:5]
    last = [slot for slot, axis in zip(came_slots(counts), moved_axes(counts)) if axis != 0]
    came_refs, refs = refs[5 : 5 + len(last)], refs[5 + len(last) :]
    own_ref, send_refs = refs[0], refs[1 : 1 + moves]
    values_ref, parts_ref, cut_ref = refs[1 + moves :]
    block_count = 2 * (owned_slots + 6)
    all_rows = nodes_ref.shape[0]
    elem_rows = all_rows // 4
    for first in range(0, all_rows, 8):
        ids = nodes_ref[first : first + 8, :]
        found = [values_in_ref[f, first : first + 8, :] for f in range(FIELDS)]
        for ref, slot in zip(came_refs, last):
            found = add_slot(lambda r: ref[r : r + 1, :], owned_slots + slot, ids, found)
        for f in range(FIELDS):
            values_ref[f, first : first + 8, :] = found[f]
    for first in [*range(0, elem_rows - 7, 8)] + ([elem_rows - 8] if elem_rows % 8 else []):
        at = [slice(r * elem_rows + first, r * elem_rows + first + 8) for r in range(12)]
        values = [[values_ref[f, at[a], :] for f in range(FIELDS)] for a in range(4)]
        grads = [[grads_ref[at[3 * a + j], :] for j in range(3)] for a in range(4)]
        volume = volume_ref[at[0], :]
        velgrad = [[sum(values[a][i] * grads[a][j] for a in range(4)) for j in range(3)] for i in range(3)]
        strain = [[0.5 * (velgrad[i][j] + velgrad[j][i]) if i <= j else None for j in range(3)] for i in range(3)]
        diagonal = sum(strain[i][i] * strain[i][i] for i in range(3))
        corner = sum(strain[i][j] * strain[i][j] for i, j in ((0, 1), (0, 2), (1, 2)))
        second = 0.5 * diagonal + corner
        pressure, temper, damage = [0.25 * (values[0][f] + values[1][f] + values[2][f] + values[3][f]) for f in (3, 4, 5)]
        root = jnp.exp(jnp.log(second + strain_reg) * (-1.0 / 3.0))
        twice = (1.0 - damage) * jnp.exp(-temper) * root
        stress = [[None] * 3 for _ in range(3)]
        for i in range(3):
            for j in range(i, 3):
                stress[i][j] = twice * strain[i][j] - (pressure if i == j else 0.0)
                stress[j][i] = stress[i][j]
        lift = (0.25 * gravity) * volume
        flow = 0.25 * volume * (velgrad[0][0] + velgrad[1][1] + velgrad[2][2])
        for s, part in enumerate(cut_parts(flow)):
            for a in range(4):
                parts_ref[3 * SPLITS + s, at[a], :] = part
        for a in range(4):
            for i in range(3):
                force = volume * sum(stress[i][j] * grads[a][j] for j in range(3))
                if i == 2:
                    force = force + lift
                for s, part in enumerate(cut_parts(force)):
                    parts_ref[i * SPLITS + s, at[a], :] = part

    group = node_hot_ref.shape[1] // BLOCK

    width = 4 * block_count
    total = jnp.zeros((SPLITS * width, BLOCK), jnp.float32)
    for step in range(all_rows // group):
        lefts = []
        for r in range(step * group, (step + 1) * group):
            terms = [parts_ref[c * SPLITS + s, r : r + 1, :] for s in range(SPLITS) for c in range(4)]
            lefts.append(placed(terms, nodes_ref[r : r + 1, :], block_count))
        total = total + hot_dot(jnp.concatenate(lefts, axis=1), node_hot_ref[step])
    total = sum(total[s * width : (s + 1) * width, :] for s in range(SPLITS))
    owned = 2 * owned_slots
    for c in range(4):
        own_ref[c * owned : (c + 1) * owned, :] = total[c * block_count : c * block_count + owned, :]
        for k in range(6):
            first = c * block_count + owned + 2 * k
            cut_ref[k, 2 * c : 2 * c + 2, :] = total[first : first + 2, :]
    send_pairs(counts, cut_ref, send_refs, [(1, 0), (3, 2), (5, 4)])


def placed_few(values, ids, block_count):
    each = 8 // block_count
    rows = lax.broadcasted_iota(jnp.int32, (8, BLOCK), 0)
    hit = (rows & (block_count - 1)) == jnp.broadcast_to(ids >> 7, rows.shape)
    left = []
    for first in range(0, len(values), each):
        tile = jnp.broadcast_to(values[first], rows.shape)
        for i in range(1, each):
            tile = jnp.where(rows >= i * block_count, jnp.broadcast_to(values[first + i], rows.shape), tile)
        left.append(jnp.where(hit, tile, 0.0))
    return jnp.concatenate(left, axis=0).astype(jnp.bfloat16)


def add_returned(total, came_refs, directions, halos_ref, halo_hot_ref):
    owned = total.shape[0] // 4
    lefts, rights = [], []
    for ref, k in zip(came_refs, directions):
        parts = cut_parts(ref[...])
        for h in range(2):
            terms = [parts[s][2 * c + h : 2 * c + h + 1, :] for s in range(SPLITS) for c in range(4)]
            lefts.append(placed_few(terms, halos_ref[pl.ds(2 * k + h, 1), :], owned))
            rights.append(halo_hot_ref[pl.ds(pl.multiple_of((2 * k + h) * BLOCK, BLOCK), BLOCK), :])
    sums = hot_dot(jnp.concatenate(lefts, axis=1), jnp.concatenate(rights, axis=0))
    width = 4 * owned
    return total + sum(sums[s * width : (s + 1) * width, :] for s in range(SPLITS))


def back_directions(counts):
    places = pair_places()
    long = [axis for axis in range(3) if counts[axis] > 2]
    return [2 * axis + 1 - places[axis] for axis in long] + [2 * axis + places[axis] for axis in range(3)]


def early_residual_kernel(counts, own_ref, halos_ref, halo_hot_ref, state_in_ref, *refs):
    refs, state_ref = refs[:-1], refs[-1]
    state_ref[...] = state_in_ref[...]
    directions = [k for k, axis in zip(back_directions(counts), moved_axes(counts)) if axis == 0][::-1]
    refs[-1][...] = add_returned(own_ref[...], refs[:-1], directions, halos_ref, halo_hot_ref)


def residual_kernel(counts, sums_ref, halos_ref, halo_hot_ref, *refs):
    directions = [k for k, axis in zip(back_directions(counts), moved_axes(counts)) if axis != 0]
    total = add_returned(sums_ref[...], refs[:-1], directions, halos_ref, halo_hot_ref)
    owned = total.shape[0] // 4
    for c in range(4):
        for b in range(owned):
            r = c * owned + b
            refs[-1][c : c + 1, b * BLOCK : (b + 1) * BLOCK] = total[r : r + 1, :]


def shaped(*shape):
    return jax.ShapeDtypeStruct(shape, jnp.float32)


def per_device(
    sizes,
    old_state,
    send_blocks,
    node_slots,
    node_weights,
    front_mask,
    halo_lists,
    elem_nodes,
    shape_grads,
    elem_volume,
):
    old_state, send_blocks = old_state[0, 0, 0], send_blocks[0, 0, 0]
    slots = send_blocks.shape[1]
    send_blocks = send_blocks.reshape(-1, 1, slots)
    rows = FIELDS * slots
    arguments = [
        node_slots[0, 0, 0],
        node_weights[0, 0, 0],
        front_mask.reshape(-1, BLOCK),
        halo_lists.reshape(halo_lists.shape[-2], 1, -1),
        elem_nodes[0, 0, 0],
        shape_grads.reshape(-1, BLOCK),
        elem_volume[0, 0],
        send_blocks,
    ]
    old_rows = old_state.reshape(-1, BLOCK)
    count = len(arguments)
    owned = node_slots.shape[-1]
    slot_rows = node_slots.size // BLOCK
    give_rows = 2 * rows + 2 * slot_rows
    give_first, give, old_rows, *held = pl.pallas_call(
        functools.partial(give_kernel, count),
        out_shape=[shaped(2 * rows, BLOCK), shaped(give_rows, BLOCK), shaped(*old_rows.shape)]
        + [jax.ShapeDtypeStruct(a.shape, a.dtype) for a in arguments],
        in_specs=[pl.BlockSpec(memory_space=pltpu.HBM)] * (2 + count),
        out_specs=[VMEM] * (3 + count),
        scratch_shapes=[pltpu.SMEM(send_blocks.shape, jnp.int32), pltpu.SemaphoreType.DMA((2 + count,))],
        compiler_params=params(),
    )(*(pltpu.with_memory_space_constraint(a, pltpu.HBM) for a in (send_blocks, old_rows, *arguments)))
    node_slots, node_weights, mask_rows, halos, elem_nodes, grad_rows, volume, held_blocks = held
    first, second = pl.pallas_call(
        keep_kernel,
        out_shape=(shaped(2 * rows, BLOCK),) * 2,
        in_specs=[SMEM, VMEM],
        out_specs=(VMEM,) * 2,
        compiler_params=params(),
    )(held_blocks, old_rows)
    layers = both_ways([(0, 1)])
    got_first = lax.ppermute(give_first, "layer", layers)
    got = lax.ppermute(give, "layer", layers)
    full = [jnp.concatenate([first, got_first]), jnp.concatenate([second, got[: 2 * rows]])]
    first, second = [
        lax.ppermute(part, ("mapx", "layer"), pairs).reshape(4, rows, BLOCK)
        for part, pairs in zip(full, column_moves(sizes[0]))
    ]
    other_slots, other_weights = got[2 * rows : 2 * rows + slot_rows], got[2 * rows + slot_rows :]

    all_rows = elem_nodes.size // BLOCK
    halo_count = halos.size // BLOCK
    hot_steps = next(n for n in (8, 4, 2, 1) if all_rows % n == 0)
    whole = lambda *shape: jax.ShapeDtypeStruct(shape, jnp.int32)
    found, slots_cut, weights_cut, halos_cut, nodes_cut, volume_cut, halo_hot, node_hot = pl.pallas_call(
        own_kernel,
        out_shape=(
            shaped(2, FIELDS, slot_rows, BLOCK),
            whole(2, slot_rows, BLOCK),
            shaped(slot_rows, BLOCK),
            whole(halo_count, BLOCK),
            whole(all_rows, BLOCK),
            shaped(all_rows // 4, BLOCK),
            jax.ShapeDtypeStruct((halo_count * BLOCK, BLOCK), jnp.bfloat16),
            jax.ShapeDtypeStruct((hot_steps, all_rows // hot_steps * BLOCK, BLOCK), jnp.bfloat16),
        ),
        in_specs=[SMEM] + [VMEM] * 7,
        out_specs=(VMEM,) * 8,
        scratch_shapes=[pltpu.VMEM((2, rows, BLOCK), jnp.float32)],
        compiler_params=params(),
    )(held_blocks, old_rows, other_slots, node_slots, node_weights, halos, elem_nodes, volume)
    found = pl.pallas_call(
        early_kernel,
        out_shape=shaped(2, FIELDS, slot_rows, BLOCK),
        in_specs=[VMEM] * 3,
        out_specs=VMEM,
        compiler_params=params(),
    )(first, slots_cut, found)
    state_rows = FIELDS * owned // BLOCK
    mine, other = pl.pallas_call(
        functools.partial(late_kernel, owned // BLOCK),
        out_shape=(shaped(state_rows, BLOCK),) * 2,
        in_specs=[VMEM] * 5,
        out_specs=(VMEM,) * 2,
        compiler_params=params(),
    )(second, slots_cut, found, weights_cut, other_weights)
    other = lax.ppermute(other, "layer", layers)
    moves = 3 + sum(size > 2 for size in sizes)
    chunk = (2 * FIELDS, BLOCK)
    new_state, table, *ghosts = pl.pallas_call(
        functools.partial(state_kernel, sizes),
        out_shape=(shaped(state_rows, BLOCK), shaped(owned // (2 * BLOCK), *chunk)) + (shaped(*chunk),) * moves,
        in_specs=[VMEM] * 4,
        out_specs=(VMEM,) * (2 + moves),
        scratch_shapes=[pltpu.VMEM((6, *chunk), jnp.float32)],
        compiler_params=params(),
    )(mine, other, mask_rows, halos_cut)
    ghosts = swap_all(ghosts, sizes)

    owned_slots = table.shape[0]
    early = [ghost for ghost, axis in zip(ghosts, moved_axes(sizes)) if axis == 0]
    late = [ghost for ghost, axis in zip(ghosts, moved_axes(sizes)) if axis != 0]
    values = pl.pallas_call(
        functools.partial(values_kernel, sizes),
        out_shape=shaped(FIELDS, all_rows, BLOCK),
        in_specs=[VMEM] * (2 + len(early)),
        out_specs=VMEM,
        compiler_params=params(),
    )(table, nodes_cut, *early)
    own, *sums = pl.pallas_call(
        functools.partial(element_kernel, sizes, moves, owned_slots),
        out_shape=(shaped(4 * owned // BLOCK, BLOCK),) + (shaped(8, BLOCK),) * moves,
        in_specs=[VMEM] * (5 + len(late)),
        out_specs=(VMEM,) * (1 + moves),
        scratch_shapes=[
            pltpu.VMEM((FIELDS, all_rows, BLOCK), jnp.float32),
            pltpu.VMEM((4 * SPLITS, all_rows, BLOCK), jnp.float32),
            pltpu.VMEM((6, 8, BLOCK), jnp.float32),
        ],
        compiler_params=params(),
    )(values, nodes_cut, node_hot, grad_rows, volume_cut, *late)
    sums = swap_all(sums, sizes)
    early = [came for came, axis in zip(sums, moved_axes(sizes)) if axis == 0][::-1]
    late = [came for came, axis in zip(sums, moved_axes(sizes)) if axis != 0]
    own, new_state = pl.pallas_call(
        functools.partial(early_residual_kernel, sizes),
        out_shape=(shaped(*own.shape), shaped(*new_state.shape)),
        in_specs=[VMEM] * (4 + len(early)),
        out_specs=(VMEM,) * 2,
        compiler_params=params(),
    )(own, halos_cut, halo_hot, new_state, *early)
    residual = pl.pallas_call(
        functools.partial(residual_kernel, sizes),
        out_shape=shaped(4, owned),
        in_specs=[VMEM] * (3 + len(late)),
        out_specs=VMEM,
        compiler_params=params(),
    )(own, halos_cut, halo_hot, *late)
    return (new_state.reshape(1, 1, 1, FIELDS, owned), residual[None, None, None])


def solution(mesh):
    sizes = tuple(mesh.shape[axis] for axis in AXES)
    row = P("mapx", "mapy", "layer", None)
    table = P("mapx", "mapy", "layer", None, None)
    return jax.shard_map(
        functools.partial(per_device, sizes),
        mesh=mesh,
        in_specs=(table, table, table, table, row, table, table, table, row),
        out_specs=(table, table),
        check_vma=False,
    )
```

profile of v0, /device:TPU:0, one launch (start us, length us, event | category | flops | bytes accessed | tf_op | source)
XLA Modules:
  0.0 38.0 jit_solution(6043453008067668055)
XLA Ops:
  0.6 1.3 %shard_map.104 = (f32[192,128]{1,0:T(8,128)S(1)}, f32[224,128]{1,0:T(8,128)S(1)}, f32[384,128]{1,0:T(8,128)S(1)}, s32[4,512]{1,0:T(4,128)S(1)}, f32[4,512]{1,0:T...) custom-call(s32[10,1,16]{2,1,0:T(1,128)} %bitcast.18, ...), custom_call_target="tpu_custom_call" | custom-call | tf_op jit(solution)/shard_map/pallas_call | solution.py:492
  1.9 0.5 %collective-permute-start.2 = (f32[192,128]{1,0:T(8,128)S(1)}, f32[192,128]{1,0:T(8,128)S(1)}, u32[]{:S(2)}, u32[]{:S(2)}) collective-permute-start(f32[192,128]{1,0:T(8,128)S(1)} %get-tuple-element.49), channel_id=1, source_target_pairs={{0,1},{1,0},{2,3},{3,2},{4,5},{5,4},{6,7},{7,6},{8,9},{9,8},{10,11... | collective-permute-start | bytes 294920 | tf_op jit(solution)/shard_map/ppermute | solution.py:510
  2.4 0.1 collective-permute-start
  2.5 0.8 %shard_map.105 = (f32[192,128]{1,0:T(8,128)S(1)}, f32[192,128]{1,0:T(8,128)S(1)}) custom-call(s32[10,1,16]{2,1,0:T(1,128)S(1)} %get-tuple-element.38.blocks_ref, f32[384,128]{1,0:T(8,128)S(1)} %get-tuple-element.39.old_ref), custom_call_target="tpu_custom_call" | custom-call | tf_op jit(solution)/shard_map/pallas_call | solution.py:502
  3.3 0.0 collective-permute-done.2
  3.4 4.8 %collective-permute-start.3 = (f32[384,128]{1,0:T(8,128)S(1)}, f32[384,128]{1,0:T(8,128)S(1)}, u32[]{:S(2)}, u32[]{:S(2)}) collective-permute-start(f32[384,128]{1,0:T(8,128)S(1)} %pad_maximum_fusion.1), channel_id=1, source_target_pairs={{5,9},{9,5},{13,17},{17,13},{21,25},{25,21},{0,4},{4,0},{8,12},{12... | collective-permute-start | bytes 589832 | tf_op jit(solution)/shard_map/ppermute | solution.py:514
  8.3 3.5 %collective-permute-start.1 = (f32[384,128]{1,0:T(8,128)S(1)}, f32[384,128]{1,0:T(8,128)S(1)}, u32[]{:S(2)}, u32[]{:S(2)}) collective-permute-start(f32[384,128]{1,0:T(8,128)S(1)} %pad_maximum_fusion), channel_id=1, source_target_pairs={{0,8},{8,0},{4,12},{12,4},{16,24},{24,16},{20,28},{28,20},{9,17},{... | collective-permute-start | bytes 589832 | tf_op jit(solution)/shard_map/ppermute | solution.py:514
  11.8 2.7 %shard_map.106 = (f32[2,6,16,128]{3,2,1,0:T(8,128)S(1)}, s32[2,16,128]{2,1,0:T(8,128)S(1)}, f32[16,128]{1,0:T(8,128)S(1)}, s32[12,128]{1,0:T(8,128)S(1)}, s32[80...) custom-call(s32[10,1,16]{2,1,0:T(1,128)S(1)} %get-tuple-element.38.b, ...), custom_call_target="tpu_custom_call" | custom-call | tf_op jit(solution)/shard_map/pallas_call | solution.py:523
  14.5 0.0 collective-permute-done.3
  14.5 0.9 %shard_map.107.found_ref = f32[2,6,16,128]{3,2,1,0:T(8,128)S(1)} custom-call(f32[4,96,128]{2,1,0:T(8,128)S(1)} %bitcast.13, s32[2,16,128]{2,1,0:T(8,128)S(1)} %get-tuple-element.47.slots_ref, f32[2,6,16,128]{3,2,1,0:T(8,128)S(1)} %get-tuple-element.50.found_in_ref), custom_call_target="tpu_custom_call" | custom-call | tf_op jit(solution)/shard_map/pallas_call | solution.py:540
  15.4 0.5 %collective-permute-done.1 = f32[384,128]{1,0:T(8,128)S(1)} collective-permute-done((f32[384,128]{1,0:T(8,128)S(1)}, f32[384,128]{1,0:T(8,128)S(1)}, u32[]{:S(2)}, u32[]{:S(2)}) %collective-permute-start.1) | collective-permute-done | bytes 196640 | tf_op jit(solution)/shard_map/ppermute | solution.py:514
  15.8 0.9 %shard_map.108 = (f32[24,128]{1,0:T(8,128)S(1)}, f32[24,128]{1,0:T(8,128)S(1)}) custom-call(f32[4,96,128]{2,1,0:T(8,128)S(1)} %bitcast.14, s32[2,16,128]{2,1,0:T(8,128)S(1)} %get-tuple-element.47.slots_ref, f32[2,6,16,128]{3,2,1,0:T(8,128)S(1)} %shard_map.107.found_ref, f32[16,128]{1,0:T(8,128)S(1)} %get-tuple-element.51.weights_ref, ...), custom_call_target="tpu_custom_call" | custom-call | tf_op jit(solution)/shard_map/pallas_call | solution.py:548
  16.7 0.1 collective-permute-start.4
  16.8 1.2 %collective-permute-done.4.came_ref = f32[24,128]{1,0:T(8,128)S(1)} collective-permute-done((f32[24,128]{1,0:T(8,128)S(1)}, f32[24,128]{1,0:T(8,128)S(1)}, u32[]{:S(2)}, u32[]{:S(2)}) %collective-permute-start.4) | collective-permute-done | bytes 12320 | tf_op jit(solution)/shard_map/ppermute | solution.py:555
  18.0 0.1 shard_map.109
  18.1 0.7 %collective-permute-start.5 = (f32[12,128]{1,0:T(8,128)S(1)}, f32[12,128]{1,0:T(8,128)S(1)}, u32[]{:S(2)}, u32[]{:S(2)}) collective-permute-start(f32[12,128]{1,0:T(8,128)S(1)} %get-tuple-element.58), channel_id=1, source_target_pairs={{4,8},{8,4},{12,16},{16,12},{20,24},{24,20},{5,9},{9,5},{13,17},{1... | collective-permute-start | bytes 18440 | tf_op jit(solution)/shard_map/ppermute | solution.py:52
  18.8 4.4 %collective-permute-start.6 = (f32[12,128]{1,0:T(8,128)S(1)}, f32[12,128]{1,0:T(8,128)S(1)}, u32[]{:S(2)}, u32[]{:S(2)}) collective-permute-start(f32[12,128]{1,0:T(8,128)S(1)} %get-tuple-element.59), channel_id=1, source_target_pairs={{0,4},{4,0},{8,12},{12,8},{16,20},{20,16},{24,28},{28,24},{1,5},{5... | collective-permute-start | bytes 18440 | tf_op jit(solution)/shard_map/ppermute | solution.py:52
  23.1 1.5 %collective-permute-start.7 = (f32[12,128]{1,0:T(8,128)S(1)}, f32[12,128]{1,0:T(8,128)S(1)}, u32[]{:S(2)}, u32[]{:S(2)}) collective-permute-start(f32[12,128]{1,0:T(8,128)S(1)} %get-tuple-element.63), channel_id=1, source_target_pairs={{0,2},{2,0},{1,3},{3,1},{4,6},{6,4},{5,7},{7,5},{8,10},{10,8},{9,1... | collective-permute-start | bytes 18440 | tf_op jit(solution)/shard_map/ppermute | solution.py:52
  24.6 0.0 collective-permute-done.5.refs_0_
  24.6 0.1 collective-permute-done.6.refs_1_
  24.8 0.6 %shard_map.110.refs_0_ = f32[6,80,128]{2,1,0:T(8,128)S(1)} custom-call(f32[2,12,128]{2,1,0:T(8,128)S(1)} %get-tuple-element.56.table_ref, s32[80,128]{1,0:T(8,128)S(1)} %get-tuple-element.57.nodes_ref.refs_1_, f32[12,128]{1,0:T(8,128)S(1)} %collective-permute-done.5.refs_0_, f32[12,128]{1,0:T(8,128)S(1)} %collective-permute-done.6.refs_1_), custom_call_target="tpu_custom_call" | custom-call | tf_op jit(solution)/shard_map/pallas_call | solution.py:571
  25.4 1.4 %collective-permute-done.7.refs_5_ = f32[12,128]{1,0:T(8,128)S(1)} collective-permute-done((f32[12,128]{1,0:T(8,128)S(1)}, f32[12,128]{1,0:T(8,128)S(1)}, u32[]{:S(2)}, u32[]{:S(2)}) %collective-permute-start.7) | collective-permute-done | bytes 6176 | tf_op jit(solution)/shard_map/ppermute | solution.py:52
  26.8 0.0 collective-permute-done.8.refs_6_
  26.8 1.8 %shard_map.111 = (f32[16,128]{1,0:T(8,128)S(1)}, f32[8,128]{1,0:T(8,128)S(1)}, f32[8,128]{1,0:T(8,128)S(1)}, f32[8,128]{1,0:T(8,128)S(1)}, f32[8,128]{1,0:T(8,128)S(1)}) custom-call(f32[6,80,128]{2,1,0:T(8,128)S(1)} %shard_map.110.refs_0_, s32[80,128]{1,0:T(8,128)S(1)} %get-tuple-element.57.nodes_ref.refs_1_, ...), custom_call_target="tpu_custom_call" | custom-call | tf_op jit(solution)/shard_map/pallas_call | solution.py:578
  28.6 0.7 %collective-permute-start.10 = (f32[8,128]{1,0:T(8,128)S(1)}, f32[8,128]{1,0:T(8,128)S(1)}, u32[]{:S(2)}, u32[]{:S(2)}) collective-permute-start(f32[8,128]{1,0:T(8,128)S(1)} %get-tuple-element.69), channel_id=1, source_target_pairs={{4,8},{8,4},{12,16},{16,12},{20,24},{24,20},{5,9},{9,5},{13,17},{1... | collective-permute-start | bytes 12296 | tf_op jit(solution)/shard_map/ppermute | solution.py:52
  29.3 4.4 %collective-permute-start.9 = (f32[8,128]{1,0:T(8,128)S(1)}, f32[8,128]{1,0:T(8,128)S(1)}, u32[]{:S(2)}, u32[]{:S(2)}) collective-permute-start(f32[8,128]{1,0:T(8,128)S(1)} %get-tuple-element.68), channel_id=1, source_target_pairs={{0,4},{4,0},{8,12},{12,8},{16,20},{20,16},{24,28},{28,24},{1,5},{5... | collective-permute-start | bytes 12296 | tf_op jit(solution)/shard_map/ppermute | solution.py:52
  33.6 1.5 %collective-permute-start.11 = (f32[8,128]{1,0:T(8,128)S(1)}, f32[8,128]{1,0:T(8,128)S(1)}, u32[]{:S(2)}, u32[]{:S(2)}) collective-permute-start(f32[8,128]{1,0:T(8,128)S(1)} %get-tuple-element.72), channel_id=1, source_target_pairs={{0,2},{2,0},{1,3},{3,1},{4,6},{6,4},{5,7},{7,5},{8,10},{10,8},{9,1... | collective-permute-start | bytes 12296 | tf_op jit(solution)/shard_map/ppermute | solution.py:52
  35.1 0.0 collective-permute-start.12
  35.1 0.1 collective-permute-done.9.refs_0_
  35.2 0.6 %shard_map.112 = (f32[16,128]{1,0:T(8,128)S(1)}, f32[24,128]{1,0:T(8,128)}) custom-call(f32[16,128]{1,0:T(8,128)S(1)} %get-tuple-element.65.own_ref, s32[12,128]{1,0:T(8,128)S(1)} %get-tuple-element.55.halos_ref, bf16[1536,128]{1,0:T(8,128)(2,1)S(1)} %get-tuple-element.66.halo_hot_ref, f32[24,128]{1,0:T(8,128)S(1)} %get-tuple-element.67.state_in_ref, ...), custom_call_target="tpu_custom_call" | custom-call | tf_op jit(solution)/shard_map/pallas_call | solution.py:593
  35.8 1.4 %collective-permute-done.11.refs_0_ = f32[8,128]{1,0:T(8,128)S(1)} collective-permute-done((f32[8,128]{1,0:T(8,128)S(1)}, f32[8,128]{1,0:T(8,128)S(1)}, u32[]{:S(2)}, u32[]{:S(2)}) %collective-permute-start.11) | collective-permute-done | bytes 4128 | tf_op jit(solution)/shard_map/ppermute | solution.py:52
  37.2 0.8 %shard_map.113 = f32[4,512]{1,0:T(4,128)} custom-call(f32[16,128]{1,0:T(8,128)S(1)} %get-tuple-element.71.sums_ref, s32[12,128]{1,0:T(8,128)S(1)} %get-tuple-element.55.halos_ref, bf16[1536,128]{1,0:T(8,128)(2,1)S(1)} %get-tuple-element.66.halo_hot_ref, f32[8,128]{1,0:T(8,128)S(1)} %collective-permute-done.11.refs_0_, ...), custom_call_target="tpu_custom_call" | custom-call | tf_op jit(solution)/shard_map/pallas_call | solution.py:600
  (8 shorter events, 0.1 us)
Async XLA Ops:
  1.9 1.5 %collective-permute-start.2 = (f32[192,128]{1,0:T(8,128)S(1)}, f32[192,128]{1,0:T(8,128)S(1)}, u32[]{:S(2)}, u32[]{:S(2)}) collective-permute-start(f32[192,128]{1,0:T(8,128)S(1)} %get-tuple-element.49), channel_id=1, source_target_pairs={{0,1},{1,0},{2,3},{3,2},{4,5},{5,4},{6,7},{7,6},{8,9},{9,8},{10,11... | collective-permute-start | bytes 294920 | tf_op jit(solution)/shard_map/ppermute | solution.py:510
  2.4 5.8 %collective-permute-start = (f32[224,128]{1,0:T(8,128)S(1)}, f32[224,128]{1,0:T(8,128)S(1)}, u32[]{:S(2)}, u32[]{:S(2)}) collective-permute-start(f32[224,128]{1,0:T(8,128)S(1)} %get-tuple-element.41), channel_id=1, source_target_pairs={{0,1},{1,0},{2,3},{3,2},{4,5},{5,4},{6,7},{7,6},{8,9},{9,8},{10,11... | collective-permute-start | bytes 344072 | tf_op jit(solution)/shard_map/ppermute | solution.py:511
  3.4 11.1 %collective-permute-start.3 = (f32[384,128]{1,0:T(8,128)S(1)}, f32[384,128]{1,0:T(8,128)S(1)}, u32[]{:S(2)}, u32[]{:S(2)}) collective-permute-start(f32[384,128]{1,0:T(8,128)S(1)} %pad_maximum_fusion.1), channel_id=1, source_target_pairs={{5,9},{9,5},{13,17},{17,13},{21,25},{25,21},{0,4},{4,0},{8,12},{12... | collective-permute-start | bytes 589832 | tf_op jit(solution)/shard_map/ppermute | solution.py:514
  8.3 7.6 %collective-permute-start.1 = (f32[384,128]{1,0:T(8,128)S(1)}, f32[384,128]{1,0:T(8,128)S(1)}, u32[]{:S(2)}, u32[]{:S(2)}) collective-permute-start(f32[384,128]{1,0:T(8,128)S(1)} %pad_maximum_fusion), channel_id=1, source_target_pairs={{0,8},{8,0},{4,12},{12,4},{16,24},{24,16},{20,28},{28,20},{9,17},{... | collective-permute-start | bytes 589832 | tf_op jit(solution)/shard_map/ppermute | solution.py:514
  16.7 1.2 %collective-permute-start.4 = (f32[24,128]{1,0:T(8,128)S(1)}, f32[24,128]{1,0:T(8,128)S(1)}, u32[]{:S(2)}, u32[]{:S(2)}) collective-permute-start(f32[24,128]{1,0:T(8,128)S(1)} %get-tuple-element.53), channel_id=1, source_target_pairs={{0,1},{1,0},{2,3},{3,2},{4,5},{5,4},{6,7},{7,6},{8,9},{9,8},{10,11... | collective-permute-start | bytes 36872 | tf_op jit(solution)/shard_map/ppermute | solution.py:555
  18.1 6.5 %collective-permute-start.5 = (f32[12,128]{1,0:T(8,128)S(1)}, f32[12,128]{1,0:T(8,128)S(1)}, u32[]{:S(2)}, u32[]{:S(2)}) collective-permute-start(f32[12,128]{1,0:T(8,128)S(1)} %get-tuple-element.58), channel_id=1, source_target_pairs={{4,8},{8,4},{12,16},{16,12},{20,24},{24,20},{5,9},{9,5},{13,17},{1... | collective-permute-start | bytes 18440 | tf_op jit(solution)/shard_map/ppermute | solution.py:52
  18.8 6.0 %collective-permute-start.6 = (f32[12,128]{1,0:T(8,128)S(1)}, f32[12,128]{1,0:T(8,128)S(1)}, u32[]{:S(2)}, u32[]{:S(2)}) collective-permute-start(f32[12,128]{1,0:T(8,128)S(1)} %get-tuple-element.59), channel_id=1, source_target_pairs={{0,4},{4,0},{8,12},{12,8},{16,20},{20,16},{24,28},{28,24},{1,5},{5... | collective-permute-start | bytes 18440 | tf_op jit(solution)/shard_map/ppermute | solution.py:52
  23.1 3.7 %collective-permute-start.7 = (f32[12,128]{1,0:T(8,128)S(1)}, f32[12,128]{1,0:T(8,128)S(1)}, u32[]{:S(2)}, u32[]{:S(2)}) collective-permute-start(f32[12,128]{1,0:T(8,128)S(1)} %get-tuple-element.63), channel_id=1, source_target_pairs={{0,2},{2,0},{1,3},{3,1},{4,6},{6,4},{5,7},{7,5},{8,10},{10,8},{9,1... | collective-permute-start | bytes 18440 | tf_op jit(solution)/shard_map/ppermute | solution.py:52
  24.6 2.1 %collective-permute-start.8 = (f32[12,128]{1,0:T(8,128)S(1)}, f32[12,128]{1,0:T(8,128)S(1)}, u32[]{:S(2)}, u32[]{:S(2)}) collective-permute-start(f32[12,128]{1,0:T(8,128)S(1)} %get-tuple-element.64), channel_id=1, source_target_pairs={{0,1},{1,0},{2,3},{3,2},{4,5},{5,4},{6,7},{7,6},{8,9},{9,8},{10,11... | collective-permute-start | bytes 18440 | tf_op jit(solution)/shard_map/ppermute | solution.py:52
  28.6 6.5 %collective-permute-start.10 = (f32[8,128]{1,0:T(8,128)S(1)}, f32[8,128]{1,0:T(8,128)S(1)}, u32[]{:S(2)}, u32[]{:S(2)}) collective-permute-start(f32[8,128]{1,0:T(8,128)S(1)} %get-tuple-element.69), channel_id=1, source_target_pairs={{4,8},{8,4},{12,16},{16,12},{20,24},{24,20},{5,9},{9,5},{13,17},{1... | collective-permute-start | bytes 12296 | tf_op jit(solution)/shard_map/ppermute | solution.py:52
  29.3 5.9 %collective-permute-start.9 = (f32[8,128]{1,0:T(8,128)S(1)}, f32[8,128]{1,0:T(8,128)S(1)}, u32[]{:S(2)}, u32[]{:S(2)}) collective-permute-start(f32[8,128]{1,0:T(8,128)S(1)} %get-tuple-element.68), channel_id=1, source_target_pairs={{0,4},{4,0},{8,12},{12,8},{16,20},{20,16},{24,28},{28,24},{1,5},{5... | collective-permute-start | bytes 12296 | tf_op jit(solution)/shard_map/ppermute | solution.py:52
  33.6 3.6 %collective-permute-start.11 = (f32[8,128]{1,0:T(8,128)S(1)}, f32[8,128]{1,0:T(8,128)S(1)}, u32[]{:S(2)}, u32[]{:S(2)}) collective-permute-start(f32[8,128]{1,0:T(8,128)S(1)} %get-tuple-element.72), channel_id=1, source_target_pairs={{0,2},{2,0},{1,3},{3,1},{4,6},{6,4},{5,7},{7,5},{8,10},{10,8},{9,1... | collective-permute-start | bytes 12296 | tf_op jit(solution)/shard_map/ppermute | solution.py:52
  35.1 2.1 %collective-permute-start.12 = (f32[8,128]{1,0:T(8,128)S(1)}, f32[8,128]{1,0:T(8,128)S(1)}, u32[]{:S(2)}, u32[]{:S(2)}) collective-permute-start(f32[8,128]{1,0:T(8,128)S(1)} %get-tuple-element.73), channel_id=1, source_target_pairs={{0,1},{1,0},{2,3},{3,2},{4,5},{5,4},{6,7},{7,6},{8,9},{9,8},{10,11... | collective-permute-start | bytes 12296 | tf_op jit(solution)/shard_map/ppermute | solution.py:52
where the time goes:
time: 38.3 us; the launch traced here: 38 us
  starting transfers between devices  22 us (57%)
  Pallas kernels  10.5 us (27%)
  waiting for transfers between devices  4.63 us (12%)
  between operations  0.77 us (2%)
    ppermute x8, starting transfers between devices, pair_swap(): lax.ppermute(value, axis, both_ways([(at, at + 1) for at in range(first,...  13.1 us
    ppermute x2, starting transfers between devices, per_device(): lax.ppermute(part, ('mapx', 'layer'), pairs).reshape(4, rows, BLOCK)  8.31 us
    ppermute x8, waiting for transfers between devices, pair_swap(): lax.ppermute(value, axis, both_ways([(at, at + 1) for at in range(first,...  2.98 us
    pallas_call x1, Pallas kernels, per_device(): pl.pallas_call(own_kernel, out_shape=(shaped(2, FIELDS, slot_rows, BLOCK)...  2.69 us
    pallas_call x1, Pallas kernels, per_device(): pl.pallas_call(functools.partial(element_kernel, sizes, moves, owned_slot...  1.82 us
    pallas_call x1, Pallas kernels, per_device(): pl.pallas_call(functools.partial(give_kernel, count), out_shape=[shaped(2...  1.26 us
    ppermute x1, waiting for transfers between devices, per_device(): other = lax.ppermute(other, 'layer', layers)  1.16 us
    pallas_call x1, Pallas kernels, per_device(): pl.pallas_call(early_kernel, out_shape=shaped(2, FIELDS, slot_rows, BLOCK...  0.89 us
  transfers between devices with their start and end apart: 13, of which 6 were waited for; matrix products, arithmetic and copies ran while one was open for 0% of the time, Pallas kernels for 15%

commit v1 on v0

--- a/solution.py
+++ b/solution.py
@@ -223,18 +223,17 @@
             save_fields(found_ref, owner, v, found)
 
 
-def late_kernel(rows, came_ref, slots_ref, found_ref, weights_ref, other_weights_ref, mine_ref, other_ref):
-    for owner, out_ref, weight_ref in ((1, other_ref, other_weights_ref), (0, mine_ref, weights_ref)):
-        totals = [jnp.zeros((rows, BLOCK), jnp.float32) for _ in range(FIELDS)]
-        for v in range(slots_ref.shape[1] // 8):
-            ids = slots_ref[owner, 8 * v : 8 * v + 8, :]
-            found = arrived_chunks(came_ref, 1, ids, load_fields(found_ref, owner, v), owner)
-            for f in range(FIELDS):
-                term = found[f] * weight_ref[8 * v : 8 * v + 8, :]
-                for k in range(8 // rows):
-                    totals[f] = totals[f] + term[k * rows : (k + 1) * rows, :]
+def late_kernel(rows, owner, came_ref, slots_ref, found_ref, weights_ref, out_ref):
+    totals = [jnp.zeros((rows, BLOCK), jnp.float32) for _ in range(FIELDS)]
+    for v in range(slots_ref.shape[1] // 8):
+        ids = slots_ref[owner, 8 * v : 8 * v + 8, :]
+        found = arrived_chunks(came_ref, 1, ids, load_fields(found_ref, owner, v), owner)
         for f in range(FIELDS):
-            out_ref[f * rows : (f + 1) * rows, :] = totals[f]
+            term = found[f] * weights_ref[8 * v : 8 * v + 8, :]
+            for k in range(8 // rows):
+                totals[f] = totals[f] + term[k * rows : (k + 1) * rows, :]
+    for f in range(FIELDS):
+        out_ref[f * rows : (f + 1) * rows, :] = totals[f]
 
 
 def state_kernel(counts, mine_ref, came_ref, mask_ref, halos_ref, state_ref, table_ref, *more_refs):
@@ -545,13 +544,16 @@
         compiler_params=params(),
     )(first, slots_cut, found)
     state_rows = FIELDS * owned // BLOCK
-    mine, other = pl.pallas_call(
-        functools.partial(late_kernel, owned // BLOCK),
-        out_shape=(shaped(state_rows, BLOCK),) * 2,
-        in_specs=[VMEM] * 5,
-        out_specs=(VMEM,) * 2,
-        compiler_params=params(),
-    )(second, slots_cut, found, weights_cut, other_weights)
+    other, mine = [
+        pl.pallas_call(
+            functools.partial(late_kernel, owned // BLOCK, owner),
+            out_shape=shaped(state_rows, BLOCK),
+            in_specs=[VMEM] * 4,
+            out_specs=VMEM,
+            compiler_params=params(),
+        )(second, slots_cut, found, weights)
+        for owner, weights in ((1, other_weights), (0, weights_cut))
+    ]
     other = lax.ppermute(other, "layer", layers)
     moves = 3 + sum(size > 2 for size in sizes)
     chunk = (2 * FIELDS, BLOCK)

time: 38.3 us -> 37.9 us (0.990)
  waiting for transfers between devices: 4.63 us -> 4.13 us
    ppermute x1, waiting for transfers between devices: 1.16 us -> 0.67 us  [per_device(): other = lax.ppermute(other, 'layer', layers)]
    pallas_call x1 -> x2, Pallas kernels: 0.89 us -> 0.96 us  [per_device(): pl.pallas_call(functools.partial(late_kernel, owned // BLOCK, owner), out...]
  transfers between devices with their start and end apart: 13 -> 13, of which waited for: 6 -> 6; matrix products, arithmetic and copies ran while one was open for 0% -> 0% of each run, Pallas kernels for 15% -> 16%
where the time goes in v1:
time: 37.9 us; the launch traced here: 37.6 us
  starting transfers between devices  22 us (58%)
  Pallas kernels  10.6 us (28%)
  waiting for transfers between devices  4.13 us (11%)
  between operations  0.78 us (2%)
    ppermute x8, starting transfers between devices, pair_swap(): lax.ppermute(value, axis, both_ways([(at, at + 1) for at in range(first,...  13.1 us
    ppermute x2, starting transfers between devices, per_device(): lax.ppermute(part, ('mapx', 'layer'), pairs).reshape(4, rows, BLOCK)  8.31 us
    ppermute x8, waiting for transfers between devices, pair_swap(): lax.ppermute(value, axis, both_ways([(at, at + 1) for at in range(first,...  2.98 us
    pallas_call x1, Pallas kernels, per_device(): pl.pallas_call(own_kernel, out_shape=(shaped(2, FIELDS, slot_rows, BLOCK)...  2.69 us
    pallas_call x1, Pallas kernels, per_device(): pl.pallas_call(functools.partial(element_kernel, sizes, moves, owned_slot...  1.81 us
    pallas_call x1, Pallas kernels, per_device(): pl.pallas_call(functools.partial(give_kernel, count), out_shape=[shaped(2...  1.26 us
    pallas_call x2, Pallas kernels, per_device(): pl.pallas_call(functools.partial(late_kernel, owned // BLOCK, owner), out...  0.96 us
    pallas_call x1, Pallas kernels, per_device(): pl.pallas_call(early_kernel, out_shape=shaped(2, FIELDS, slot_rows, BLOCK...  0.89 us
  transfers between devices with their start and end apart: 13, of which 6 were waited for; matrix products, arithmetic and copies ran while one was open for 0% of the time, Pallas kernels for 16%

profile of v1, /device:TPU:0, one launch (start us, length us, event | category | flops | bytes accessed | tf_op | source)
XLA Modules:
  0.0 37.6 jit_solution(18032324612393391977)
XLA Ops:
  0.6 1.3 %shard_map.104 = (f32[192,128]{1,0:T(8,128)S(1)}, f32[224,128]{1,0:T(8,128)S(1)}, f32[384,128]{1,0:T(8,128)S(1)}, s32[4,512]{1,0:T(4,128)S(1)}, f32[4,512]{1,0:T...) custom-call(s32[10,1,16]{2,1,0:T(1,128)} %bitcast.19, ...), custom_call_target="tpu_custom_call" | custom-call | tf_op jit(solution)/shard_map/pallas_call | solution.py:491
  1.9 0.5 %collective-permute-start.2 = (f32[192,128]{1,0:T(8,128)S(1)}, f32[192,128]{1,0:T(8,128)S(1)}, u32[]{:S(2)}, u32[]{:S(2)}) collective-permute-start(f32[192,128]{1,0:T(8,128)S(1)} %get-tuple-element.47), channel_id=1, source_target_pairs={{0,1},{1,0},{2,3},{3,2},{4,5},{5,4},{6,7},{7,6},{8,9},{9,8},{10,11... | collective-permute-start | bytes 294920 | tf_op jit(solution)/shard_map/ppermute | solution.py:509
  2.4 0.1 collective-permute-start
  2.5 0.8 %shard_map.105 = (f32[192,128]{1,0:T(8,128)S(1)}, f32[192,128]{1,0:T(8,128)S(1)}) custom-call(s32[10,1,16]{2,1,0:T(1,128)S(1)} %get-tuple-element.36.blocks_ref, f32[384,128]{1,0:T(8,128)S(1)} %get-tuple-element.37.old_ref), custom_call_target="tpu_custom_call" | custom-call | tf_op jit(solution)/shard_map/pallas_call | solution.py:501
  3.3 0.0 collective-permute-done.2
  3.4 4.8 %collective-permute-start.3 = (f32[384,128]{1,0:T(8,128)S(1)}, f32[384,128]{1,0:T(8,128)S(1)}, u32[]{:S(2)}, u32[]{:S(2)}) collective-permute-start(f32[384,128]{1,0:T(8,128)S(1)} %pad_maximum_fusion.1), channel_id=1, source_target_pairs={{5,9},{9,5},{13,17},{17,13},{21,25},{25,21},{0,4},{4,0},{8,12},{12... | collective-permute-start | bytes 589832 | tf_op jit(solution)/shard_map/ppermute | solution.py:513
  8.3 3.5 %collective-permute-start.1 = (f32[384,128]{1,0:T(8,128)S(1)}, f32[384,128]{1,0:T(8,128)S(1)}, u32[]{:S(2)}, u32[]{:S(2)}) collective-permute-start(f32[384,128]{1,0:T(8,128)S(1)} %pad_maximum_fusion), channel_id=1, source_target_pairs={{0,8},{8,0},{4,12},{12,4},{16,24},{24,16},{20,28},{28,20},{9,17},{... | collective-permute-start | bytes 589832 | tf_op jit(solution)/shard_map/ppermute | solution.py:513
  11.8 2.7 %shard_map.106 = (f32[2,6,16,128]{3,2,1,0:T(8,128)S(1)}, s32[2,16,128]{2,1,0:T(8,128)S(1)}, f32[16,128]{1,0:T(8,128)S(1)}, s32[12,128]{1,0:T(8,128)S(1)}, s32[80...) custom-call(s32[10,1,16]{2,1,0:T(1,128)S(1)} %get-tuple-element.36.b, ...), custom_call_target="tpu_custom_call" | custom-call | tf_op jit(solution)/shard_map/pallas_call | solution.py:522
  14.5 0.0 collective-permute-done.3
  14.5 0.9 %shard_map.107.found_ref = f32[2,6,16,128]{3,2,1,0:T(8,128)S(1)} custom-call(f32[4,96,128]{2,1,0:T(8,128)S(1)} %bitcast.15, s32[2,16,128]{2,1,0:T(8,128)S(1)} %get-tuple-element.45.slots_ref, f32[2,6,16,128]{3,2,1,0:T(8,128)S(1)} %get-tuple-element.48.found_in_ref), custom_call_target="tpu_custom_call" | custom-call | tf_op jit(solution)/shard_map/pallas_call | solution.py:539
  15.4 0.5 %collective-permute-done.1 = f32[384,128]{1,0:T(8,128)S(1)} collective-permute-done((f32[384,128]{1,0:T(8,128)S(1)}, f32[384,128]{1,0:T(8,128)S(1)}, u32[]{:S(2)}, u32[]{:S(2)}) %collective-permute-start.1) | collective-permute-done | bytes 196640 | tf_op jit(solution)/shard_map/ppermute | solution.py:513
  15.8 0.5 %shard_map.109 = f32[24,128]{1,0:T(8,128)S(1)} custom-call(f32[4,96,128]{2,1,0:T(8,128)S(1)} %bitcast.13, s32[2,16,128]{2,1,0:T(8,128)S(1)} %get-tuple-element.45.slots_ref, f32[2,6,16,128]{3,2,1,0:T(8,128)S(1)} %shard_map.107.found_ref, f32[16,128]{1,0:T(8,128)S(1)} %get-tuple-element.74.weights_ref), custom_call_target="tpu_custom_call" | custom-call | tf_op jit(solution)/shard_map/pallas_call | solution.py:548
  16.3 0.1 collective-permute-start.4
  16.4 0.5 %shard_map.108.mine_ref = f32[24,128]{1,0:T(8,128)S(1)} custom-call(f32[4,96,128]{2,1,0:T(8,128)S(1)} %bitcast.14, s32[2,16,128]{2,1,0:T(8,128)S(1)} %get-tuple-element.45.slots_ref, f32[2,6,16,128]{3,2,1,0:T(8,128)S(1)} %shard_map.107.found_ref, f32[16,128]{1,0:T(8,128)S(1)} %get-tuple-element.49.weights_ref), custom_call_target="tpu_custom_call" | custom-call | tf_op jit(solution)/shard_map/pallas_call | solution.py:548
  16.9 0.7 %collective-permute-done.4.came_ref = f32[24,128]{1,0:T(8,128)S(1)} collective-permute-done((f32[24,128]{1,0:T(8,128)S(1)}, f32[24,128]{1,0:T(8,128)S(1)}, u32[]{:S(2)}, u32[]{:S(2)}) %collective-permute-start.4) | collective-permute-done | bytes 12320 | tf_op jit(solution)/shard_map/ppermute | solution.py:557
  17.6 0.1 shard_map.110
  17.7 0.7 %collective-permute-start.5 = (f32[12,128]{1,0:T(8,128)S(1)}, f32[12,128]{1,0:T(8,128)S(1)}, u32[]{:S(2)}, u32[]{:S(2)}) collective-permute-start(f32[12,128]{1,0:T(8,128)S(1)} %get-tuple-element.54), channel_id=1, source_target_pairs={{4,8},{8,4},{12,16},{16,12},{20,24},{24,20},{5,9},{9,5},{13,17},{1... | collective-permute-start | bytes 18440 | tf_op jit(solution)/shard_map/ppermute | solution.py:52
  18.4 4.4 %collective-permute-start.6 = (f32[12,128]{1,0:T(8,128)S(1)}, f32[12,128]{1,0:T(8,128)S(1)}, u32[]{:S(2)}, u32[]{:S(2)}) collective-permute-start(f32[12,128]{1,0:T(8,128)S(1)} %get-tuple-element.55), channel_id=1, source_target_pairs={{0,4},{4,0},{8,12},{12,8},{16,20},{20,16},{24,28},{28,24},{1,5},{5... | collective-permute-start | bytes 18440 | tf_op jit(solution)/shard_map/ppermute | solution.py:52
  22.7 1.5 %collective-permute-start.7 = (f32[12,128]{1,0:T(8,128)S(1)}, f32[12,128]{1,0:T(8,128)S(1)}, u32[]{:S(2)}, u32[]{:S(2)}) collective-permute-start(f32[12,128]{1,0:T(8,128)S(1)} %get-tuple-element.59), channel_id=1, source_target_pairs={{0,2},{2,0},{1,3},{3,1},{4,6},{6,4},{5,7},{7,5},{8,10},{10,8},{9,1... | collective-permute-start | bytes 18440 | tf_op jit(solution)/shard_map/ppermute | solution.py:52
  24.2 0.1 collective-permute-done.6.refs_1_
  24.3 0.6 %shard_map.111.refs_0_ = f32[6,80,128]{2,1,0:T(8,128)S(1)} custom-call(f32[2,12,128]{2,1,0:T(8,128)S(1)} %get-tuple-element.52.table_ref, s32[80,128]{1,0:T(8,128)S(1)} %get-tuple-element.53.nodes_ref.refs_1_, f32[12,128]{1,0:T(8,128)S(1)} %collective-permute-done.5.refs_0_, f32[12,128]{1,0:T(8,128)S(1)} %collective-permute-done.6.refs_1_), custom_call_target="tpu_custom_call" | custom-call | tf_op jit(solution)/shard_map/pallas_call | solution.py:573
  24.9 1.4 %collective-permute-done.7.refs_5_ = f32[12,128]{1,0:T(8,128)S(1)} collective-permute-done((f32[12,128]{1,0:T(8,128)S(1)}, f32[12,128]{1,0:T(8,128)S(1)}, u32[]{:S(2)}, u32[]{:S(2)}) %collective-permute-start.7) | collective-permute-done | bytes 6176 | tf_op jit(solution)/shard_map/ppermute | solution.py:52
  26.4 1.8 %shard_map.112 = (f32[16,128]{1,0:T(8,128)S(1)}, f32[8,128]{1,0:T(8,128)S(1)}, f32[8,128]{1,0:T(8,128)S(1)}, f32[8,128]{1,0:T(8,128)S(1)}, f32[8,128]{1,0:T(8,128)S(1)}) custom-call(f32[6,80,128]{2,1,0:T(8,128)S(1)} %shard_map.111.refs_0_, s32[80,128]{1,0:T(8,128)S(1)} %get-tuple-element.53.nodes_ref.refs_1_, ...), custom_call_target="tpu_custom_call" | custom-call | tf_op jit(solution)/shard_map/pallas_call | solution.py:580
  28.2 0.7 %collective-permute-start.10 = (f32[8,128]{1,0:T(8,128)S(1)}, f32[8,128]{1,0:T(8,128)S(1)}, u32[]{:S(2)}, u32[]{:S(2)}) collective-permute-start(f32[8,128]{1,0:T(8,128)S(1)} %get-tuple-element.65), channel_id=1, source_target_pairs={{4,8},{8,4},{12,16},{16,12},{20,24},{24,20},{5,9},{9,5},{13,17},{1... | collective-permute-start | bytes 12296 | tf_op jit(solution)/shard_map/ppermute | solution.py:52
  28.8 4.3 %collective-permute-start.9 = (f32[8,128]{1,0:T(8,128)S(1)}, f32[8,128]{1,0:T(8,128)S(1)}, u32[]{:S(2)}, u32[]{:S(2)}) collective-permute-start(f32[8,128]{1,0:T(8,128)S(1)} %get-tuple-element.64), channel_id=1, source_target_pairs={{0,4},{4,0},{8,12},{12,8},{16,20},{20,16},{24,28},{28,24},{1,5},{5... | collective-permute-start | bytes 12296 | tf_op jit(solution)/shard_map/ppermute | solution.py:52
  33.2 1.5 %collective-permute-start.11 = (f32[8,128]{1,0:T(8,128)S(1)}, f32[8,128]{1,0:T(8,128)S(1)}, u32[]{:S(2)}, u32[]{:S(2)}) collective-permute-start(f32[8,128]{1,0:T(8,128)S(1)} %get-tuple-element.68), channel_id=1, source_target_pairs={{0,2},{2,0},{1,3},{3,1},{4,6},{6,4},{5,7},{7,5},{8,10},{10,8},{9,1... | collective-permute-start | bytes 12296 | tf_op jit(solution)/shard_map/ppermute | solution.py:52
  34.7 0.0 collective-permute-start.12
  34.7 0.0 collective-permute-done.10.refs_1_
  34.7 0.1 collective-permute-done.9.refs_0_
  34.8 0.6 %shard_map.113 = (f32[16,128]{1,0:T(8,128)S(1)}, f32[24,128]{1,0:T(8,128)}) custom-call(f32[16,128]{1,0:T(8,128)S(1)} %get-tuple-element.61.own_ref, s32[12,128]{1,0:T(8,128)S(1)} %get-tuple-element.51.halos_ref, bf16[1536,128]{1,0:T(8,128)(2,1)S(1)} %get-tuple-element.62.halo_hot_ref, f32[24,128]{1,0:T(8,128)S(1)} %get-tuple-element.63.state_in_ref, ...), custom_call_target="tpu_custom_call" | custom-call | tf_op jit(solution)/shard_map/pallas_call | solution.py:595
  35.4 1.4 %collective-permute-done.11.refs_0_ = f32[8,128]{1,0:T(8,128)S(1)} collective-permute-done((f32[8,128]{1,0:T(8,128)S(1)}, f32[8,128]{1,0:T(8,128)S(1)}, u32[]{:S(2)}, u32[]{:S(2)}) %collective-permute-start.11) | collective-permute-done | bytes 4128 | tf_op jit(solution)/shard_map/ppermute | solution.py:52
  36.8 0.8 %shard_map.114 = f32[4,512]{1,0:T(4,128)} custom-call(f32[16,128]{1,0:T(8,128)S(1)} %get-tuple-element.67.sums_ref, s32[12,128]{1,0:T(8,128)S(1)} %get-tuple-element.51.halos_ref, bf16[1536,128]{1,0:T(8,128)(2,1)S(1)} %get-tuple-element.62.halo_hot_ref, f32[8,128]{1,0:T(8,128)S(1)} %collective-permute-done.11.refs_0_, ...), custom_call_target="tpu_custom_call" | custom-call | tf_op jit(solution)/shard_map/pallas_call | solution.py:602
  (9 shorter events, 0.1 us)
Async XLA Ops:
  1.9 1.5 %collective-permute-start.2 = (f32[192,128]{1,0:T(8,128)S(1)}, f32[192,128]{1,0:T(8,128)S(1)}, u32[]{:S(2)}, u32[]{:S(2)}) collective-permute-start(f32[192,128]{1,0:T(8,128)S(1)} %get-tuple-element.47), channel_id=1, source_target_pairs={{0,1},{1,0},{2,3},{3,2},{4,5},{5,4},{6,7},{7,6},{8,9},{9,8},{10,11... | collective-permute-start | bytes 294920 | tf_op jit(solution)/shard_map/ppermute | solution.py:509
  2.4 5.8 %collective-permute-start = (f32[224,128]{1,0:T(8,128)S(1)}, f32[224,128]{1,0:T(8,128)S(1)}, u32[]{:S(2)}, u32[]{:S(2)}) collective-permute-start(f32[224,128]{1,0:T(8,128)S(1)} %get-tuple-element.39), channel_id=1, source_target_pairs={{0,1},{1,0},{2,3},{3,2},{4,5},{5,4},{6,7},{7,6},{8,9},{9,8},{10,11... | collective-permute-start | bytes 344072 | tf_op jit(solution)/shard_map/ppermute | solution.py:510
  3.4 11.1 %collective-permute-start.3 = (f32[384,128]{1,0:T(8,128)S(1)}, f32[384,128]{1,0:T(8,128)S(1)}, u32[]{:S(2)}, u32[]{:S(2)}) collective-permute-start(f32[384,128]{1,0:T(8,128)S(1)} %pad_maximum_fusion.1), channel_id=1, source_target_pairs={{5,9},{9,5},{13,17},{17,13},{21,25},{25,21},{0,4},{4,0},{8,12},{12... | collective-permute-start | bytes 589832 | tf_op jit(solution)/shard_map/ppermute | solution.py:513
  8.3 7.6 %collective-permute-start.1 = (f32[384,128]{1,0:T(8,128)S(1)}, f32[384,128]{1,0:T(8,128)S(1)}, u32[]{:S(2)}, u32[]{:S(2)}) collective-permute-start(f32[384,128]{1,0:T(8,128)S(1)} %pad_maximum_fusion), channel_id=1, source_target_pairs={{0,8},{8,0},{4,12},{12,4},{16,24},{24,16},{20,28},{28,20},{9,17},{... | collective-permute-start | bytes 589832 | tf_op jit(solution)/shard_map/ppermute | solution.py:513
  16.3 1.2 %collective-permute-start.4 = (f32[24,128]{1,0:T(8,128)S(1)}, f32[24,128]{1,0:T(8,128)S(1)}, u32[]{:S(2)}, u32[]{:S(2)}) collective-permute-start(f32[24,128]{1,0:T(8,128)S(1)} %shard_map.109), channel_id=1, source_target_pairs={{0,1},{1,0},{2,3},{3,2},{4,5},{5,4},{6,7},{7,6},{8,9},{9,8},{10,11... | collective-permute-start | bytes 36872 | tf_op jit(solution)/shard_map/ppermute | solution.py:557
  17.7 6.5 %collective-permute-start.5 = (f32[12,128]{1,0:T(8,128)S(1)}, f32[12,128]{1,0:T(8,128)S(1)}, u32[]{:S(2)}, u32[]{:S(2)}) collective-permute-start(f32[12,128]{1,0:T(8,128)S(1)} %get-tuple-element.54), channel_id=1, source_target_pairs={{4,8},{8,4},{12,16},{16,12},{20,24},{24,20},{5,9},{9,5},{13,17},{1... | collective-permute-start | bytes 18440 | tf_op jit(solution)/shard_map/ppermute | solution.py:52
  18.4 6.0 %collective-permute-start.6 = (f32[12,128]{1,0:T(8,128)S(1)}, f32[12,128]{1,0:T(8,128)S(1)}, u32[]{:S(2)}, u32[]{:S(2)}) collective-permute-start(f32[12,128]{1,0:T(8,128)S(1)} %get-tuple-element.55), channel_id=1, source_target_pairs={{0,4},{4,0},{8,12},{12,8},{16,20},{20,16},{24,28},{28,24},{1,5},{5... | collective-permute-start | bytes 18440 | tf_op jit(solution)/shard_map/ppermute | solution.py:52
  22.7 3.7 %collective-permute-start.7 = (f32[12,128]{1,0:T(8,128)S(1)}, f32[12,128]{1,0:T(8,128)S(1)}, u32[]{:S(2)}, u32[]{:S(2)}) collective-permute-start(f32[12,128]{1,0:T(8,128)S(1)} %get-tuple-element.59), channel_id=1, source_target_pairs={{0,2},{2,0},{1,3},{3,1},{4,6},{6,4},{5,7},{7,5},{8,10},{10,8},{9,1... | collective-permute-start | bytes 18440 | tf_op jit(solution)/shard_map/ppermute | solution.py:52
  24.2 2.1 %collective-permute-start.8 = (f32[12,128]{1,0:T(8,128)S(1)}, f32[12,128]{1,0:T(8,128)S(1)}, u32[]{:S(2)}, u32[]{:S(2)}) collective-permute-start(f32[12,128]{1,0:T(8,128)S(1)} %get-tuple-element.60), channel_id=1, source_target_pairs={{0,1},{1,0},{2,3},{3,2},{4,5},{5,4},{6,7},{7,6},{8,9},{9,8},{10,11... | collective-permute-start | bytes 18440 | tf_op jit(solution)/shard_map/ppermute | solution.py:52
  28.2 6.5 %collective-permute-start.10 = (f32[8,128]{1,0:T(8,128)S(1)}, f32[8,128]{1,0:T(8,128)S(1)}, u32[]{:S(2)}, u32[]{:S(2)}) collective-permute-start(f32[8,128]{1,0:T(8,128)S(1)} %get-tuple-element.65), channel_id=1, source_target_pairs={{4,8},{8,4},{12,16},{16,12},{20,24},{24,20},{5,9},{9,5},{13,17},{1... | collective-permute-start | bytes 12296 | tf_op jit(solution)/shard_map/ppermute | solution.py:52
  28.8 5.9 %collective-permute-start.9 = (f32[8,128]{1,0:T(8,128)S(1)}, f32[8,128]{1,0:T(8,128)S(1)}, u32[]{:S(2)}, u32[]{:S(2)}) collective-permute-start(f32[8,128]{1,0:T(8,128)S(1)} %get-tuple-element.64), channel_id=1, source_target_pairs={{0,4},{4,0},{8,12},{12,8},{16,20},{20,16},{24,28},{28,24},{1,5},{5... | collective-permute-start | bytes 12296 | tf_op jit(solution)/shard_map/ppermute | solution.py:52
  33.2 3.6 %collective-permute-start.11 = (f32[8,128]{1,0:T(8,128)S(1)}, f32[8,128]{1,0:T(8,128)S(1)}, u32[]{:S(2)}, u32[]{:S(2)}) collective-permute-start(f32[8,128]{1,0:T(8,128)S(1)} %get-tuple-element.68), channel_id=1, source_target_pairs={{0,2},{2,0},{1,3},{3,1},{4,6},{6,4},{5,7},{7,5},{8,10},{10,8},{9,1... | collective-permute-start | bytes 12296 | tf_op jit(solution)/shard_map/ppermute | solution.py:52
  34.7 2.1 %collective-permute-start.12 = (f32[8,128]{1,0:T(8,128)S(1)}, f32[8,128]{1,0:T(8,128)S(1)}, u32[]{:S(2)}, u32[]{:S(2)}) collective-permute-start(f32[8,128]{1,0:T(8,128)S(1)} %get-tuple-element.69), channel_id=1, source_target_pairs={{0,1},{1,0},{2,3},{3,2},{4,5},{5,4},{6,7},{7,6},{8,9},{9,8},{10,11... | collective-permute-start | bytes 12296 | tf_op jit(solution)/shard_map/ppermute | solution.py:52

commit v2 on v1

--- a/solution.py
+++ b/solution.py
@@ -36,8 +36,8 @@
     across = [(at + i, at + i + 2) for at in range(2, count - 3, 4) for i in range(2)]
     number = lambda pairs, layer: [(one * 2 + layer, other * 2 + layer) for one, other in pairs]
     return [
-        both_ways(number(outside, 1) + number(inside, 0)),
-        both_ways(number(within, 0) + number(across, 1)),
+        both_ways(number(outside, 1) + number(within, 0)),
+        both_ways(number(inside, 0) + number(across, 1)),
     ]
 
 
@@ -45,7 +45,7 @@
     at = lax.axis_index("mapx")
     near = jnp.where(lax.rem(at, 2) == 0, 1, -1)
     two = jnp.where(lax.rem(at, 4) < 2, 2, -2)
-    return [jnp.where(layer == 0, near, -near), jnp.where(layer == 0, two, -two)]
+    return [jnp.where(layer == 0, two, -near), jnp.where(layer == 0, near, -two)]
 
 
 def pair_swap(value, axis, count, first):

time: 37.9 us -> 37.9 us (level)
  transfers between devices with their start and end apart: 13 -> 13, of which waited for: 6 -> 5; matrix products, arithmetic and copies ran while one was open for 0% -> 0% of each run, Pallas kernels for 16% -> 16%
where the time goes in v2:
time: 37.9 us; the launch traced here: 37.7 us
  starting transfers between devices  22.3 us (59%)
  Pallas kernels  10.6 us (28%)
  waiting for transfers between devices  3.99 us (11%)
  between operations  0.78 us (2%)
    ppermute x8, starting transfers between devices, pair_swap(): lax.ppermute(value, axis, both_ways([(at, at + 1) for at in range(first,...  13.3 us
    ppermute x2, starting transfers between devices, per_device(): lax.ppermute(part, ('mapx', 'layer'), pairs).reshape(4, rows, BLOCK)  8.31 us
    ppermute x8, waiting for transfers between devices, pair_swap(): lax.ppermute(value, axis, both_ways([(at, at + 1) for at in range(first,...  2.76 us
    pallas_call x1, Pallas kernels, per_device(): pl.pallas_call(own_kernel, out_shape=(shaped(2, FIELDS, slot_rows, BLOCK)...  2.69 us
    pallas_call x1, Pallas kernels, per_device(): pl.pallas_call(functools.partial(element_kernel, sizes, moves, owned_slot...  1.81 us
    pallas_call x1, Pallas kernels, per_device(): pl.pallas_call(functools.partial(give_kernel, count), out_shape=[shaped(2...  1.26 us
    pallas_call x2, Pallas kernels, per_device(): pl.pallas_call(functools.partial(late_kernel, owned // BLOCK, owner), out...  0.96 us
    pallas_call x1, Pallas kernels, per_device(): pl.pallas_call(early_kernel, out_shape=shaped(2, FIELDS, slot_rows, BLOCK...  0.89 us
  transfers between devices with their start and end apart: 13, of which 5 were waited for; matrix products, arithmetic and copies ran while one was open for 0% of the time, Pallas kernels for 16%

profile of v2, /device:TPU:0, one launch (start us, length us, event | category | flops | bytes accessed | tf_op | source)
XLA Modules:
  0.0 37.7 jit_solution(15650332048988154476)
XLA Ops:
  0.6 1.3 %shard_map.104 = (f32[192,128]{1,0:T(8,128)S(1)}, f32[224,128]{1,0:T(8,128)S(1)}, f32[384,128]{1,0:T(8,128)S(1)}, s32[4,512]{1,0:T(4,128)S(1)}, f32[4,512]{1,0:T...) custom-call(s32[10,1,16]{2,1,0:T(1,128)} %bitcast.19, ...), custom_call_target="tpu_custom_call" | custom-call | tf_op jit(solution)/shard_map/pallas_call | solution.py:491
  1.9 0.5 %collective-permute-start.2 = (f32[192,128]{1,0:T(8,128)S(1)}, f32[192,128]{1,0:T(8,128)S(1)}, u32[]{:S(2)}, u32[]{:S(2)}) collective-permute-start(f32[192,128]{1,0:T(8,128)S(1)} %get-tuple-element.47), channel_id=1, source_target_pairs={{0,1},{1,0},{2,3},{3,2},{4,5},{5,4},{6,7},{7,6},{8,9},{9,8},{10,11... | collective-permute-start | bytes 294920 | tf_op jit(solution)/shard_map/ppermute | solution.py:509
  2.4 0.1 collective-permute-start
  2.5 0.8 %shard_map.105 = (f32[192,128]{1,0:T(8,128)S(1)}, f32[192,128]{1,0:T(8,128)S(1)}) custom-call(s32[10,1,16]{2,1,0:T(1,128)S(1)} %get-tuple-element.36.blocks_ref, f32[384,128]{1,0:T(8,128)S(1)} %get-tuple-element.37.old_ref), custom_call_target="tpu_custom_call" | custom-call | tf_op jit(solution)/shard_map/pallas_call | solution.py:501
  3.3 0.0 collective-permute-done.2
  3.4 4.9 %collective-permute-start.3 = (f32[384,128]{1,0:T(8,128)S(1)}, f32[384,128]{1,0:T(8,128)S(1)}, u32[]{:S(2)}, u32[]{:S(2)}) collective-permute-start(f32[384,128]{1,0:T(8,128)S(1)} %pad_maximum_fusion.1), channel_id=1, source_target_pairs={{5,9},{9,5},{13,17},{17,13},{21,25},{25,21},{0,8},{8,0},{4,12},{12... | collective-permute-start | bytes 589832 | tf_op jit(solution)/shard_map/ppermute | solution.py:513
  8.3 0.0 collective-permute-done
  8.3 3.4 %collective-permute-start.1 = (f32[384,128]{1,0:T(8,128)S(1)}, f32[384,128]{1,0:T(8,128)S(1)}, u32[]{:S(2)}, u32[]{:S(2)}) collective-permute-start(f32[384,128]{1,0:T(8,128)S(1)} %pad_maximum_fusion), channel_id=1, source_target_pairs={{0,4},{4,0},{8,12},{12,8},{16,20},{20,16},{24,28},{28,24},{9,17},{... | collective-permute-start | bytes 589832 | tf_op jit(solution)/shard_map/ppermute | solution.py:513
  11.8 2.7 %shard_map.106 = (f32[2,6,16,128]{3,2,1,0:T(8,128)S(1)}, s32[2,16,128]{2,1,0:T(8,128)S(1)}, f32[16,128]{1,0:T(8,128)S(1)}, s32[12,128]{1,0:T(8,128)S(1)}, s32[80...) custom-call(s32[10,1,16]{2,1,0:T(1,128)S(1)} %get-tuple-element.36.b, ...), custom_call_target="tpu_custom_call" | custom-call | tf_op jit(solution)/shard_map/pallas_call | solution.py:522
  14.5 0.0 collective-permute-done.3
  14.5 0.9 %shard_map.107.found_ref = f32[2,6,16,128]{3,2,1,0:T(8,128)S(1)} custom-call(f32[4,96,128]{2,1,0:T(8,128)S(1)} %bitcast.15, s32[2,16,128]{2,1,0:T(8,128)S(1)} %get-tuple-element.45.slots_ref, f32[2,6,16,128]{3,2,1,0:T(8,128)S(1)} %get-tuple-element.48.found_in_ref), custom_call_target="tpu_custom_call" | custom-call | tf_op jit(solution)/shard_map/pallas_call | solution.py:539
  15.4 0.5 %collective-permute-done.1 = f32[384,128]{1,0:T(8,128)S(1)} collective-permute-done((f32[384,128]{1,0:T(8,128)S(1)}, f32[384,128]{1,0:T(8,128)S(1)}, u32[]{:S(2)}, u32[]{:S(2)}) %collective-permute-start.1) | collective-permute-done | bytes 196640 | tf_op jit(solution)/shard_map/ppermute | solution.py:513
  15.9 0.5 %shard_map.109 = f32[24,128]{1,0:T(8,128)S(1)} custom-call(f32[4,96,128]{2,1,0:T(8,128)S(1)} %bitcast.13, s32[2,16,128]{2,1,0:T(8,128)S(1)} %get-tuple-element.45.slots_ref, f32[2,6,16,128]{3,2,1,0:T(8,128)S(1)} %shard_map.107.found_ref, f32[16,128]{1,0:T(8,128)S(1)} %get-tuple-element.74.weights_ref), custom_call_target="tpu_custom_call" | custom-call | tf_op jit(solution)/shard_map/pallas_call | solution.py:548
  16.4 0.1 collective-permute-start.4
  16.5 0.5 %shard_map.108.mine_ref = f32[24,128]{1,0:T(8,128)S(1)} custom-call(f32[4,96,128]{2,1,0:T(8,128)S(1)} %bitcast.14, s32[2,16,128]{2,1,0:T(8,128)S(1)} %get-tuple-element.45.slots_ref, f32[2,6,16,128]{3,2,1,0:T(8,128)S(1)} %shard_map.107.found_ref, f32[16,128]{1,0:T(8,128)S(1)} %get-tuple-element.49.weights_ref), custom_call_target="tpu_custom_call" | custom-call | tf_op jit(solution)/shard_map/pallas_call | solution.py:548
  17.0 0.7 %collective-permute-done.4.came_ref = f32[24,128]{1,0:T(8,128)S(1)} collective-permute-done((f32[24,128]{1,0:T(8,128)S(1)}, f32[24,128]{1,0:T(8,128)S(1)}, u32[]{:S(2)}, u32[]{:S(2)}) %collective-permute-start.4) | collective-permute-done | bytes 12320 | tf_op jit(solution)/shard_map/ppermute | solution.py:557
  17.6 0.1 shard_map.110
  17.8 0.7 %collective-permute-start.5 = (f32[12,128]{1,0:T(8,128)S(1)}, f32[12,128]{1,0:T(8,128)S(1)}, u32[]{:S(2)}, u32[]{:S(2)}) collective-permute-start(f32[12,128]{1,0:T(8,128)S(1)} %get-tuple-element.54), channel_id=1, source_target_pairs={{4,8},{8,4},{12,16},{16,12},{20,24},{24,20},{5,9},{9,5},{13,17},{1... | collective-permute-start | bytes 18440 | tf_op jit(solution)/shard_map/ppermute | solution.py:52
  18.4 3.5 %collective-permute-start.6 = (f32[12,128]{1,0:T(8,128)S(1)}, f32[12,128]{1,0:T(8,128)S(1)}, u32[]{:S(2)}, u32[]{:S(2)}) collective-permute-start(f32[12,128]{1,0:T(8,128)S(1)} %get-tuple-element.55), channel_id=1, source_target_pairs={{0,4},{4,0},{8,12},{12,8},{16,20},{20,16},{24,28},{28,24},{1,5},{5... | collective-permute-start | bytes 18440 | tf_op jit(solution)/shard_map/ppermute | solution.py:52
  21.9 1.7 %collective-permute-start.7 = (f32[12,128]{1,0:T(8,128)S(1)}, f32[12,128]{1,0:T(8,128)S(1)}, u32[]{:S(2)}, u32[]{:S(2)}) collective-permute-start(f32[12,128]{1,0:T(8,128)S(1)} %get-tuple-element.59), channel_id=1, source_target_pairs={{0,2},{2,0},{1,3},{3,1},{4,6},{6,4},{5,7},{7,5},{8,10},{10,8},{9,1... | collective-permute-start | bytes 18440 | tf_op jit(solution)/shard_map/ppermute | solution.py:52
  23.6 0.0 collective-permute-start.8
  23.6 0.0 collective-permute-done.5.refs_0_
  23.7 0.6 %shard_map.111.refs_0_ = f32[6,80,128]{2,1,0:T(8,128)S(1)} custom-call(f32[2,12,128]{2,1,0:T(8,128)S(1)} %get-tuple-element.52.table_ref, s32[80,128]{1,0:T(8,128)S(1)} %get-tuple-element.53.nodes_ref.refs_1_, f32[12,128]{1,0:T(8,128)S(1)} %collective-permute-done.5.refs_0_, f32[12,128]{1,0:T(8,128)S(1)} %collective-permute-done.6.refs_1_), custom_call_target="tpu_custom_call" | custom-call | tf_op jit(solution)/shard_map/pallas_call | solution.py:573
  24.3 1.3 %collective-permute-done.7.refs_5_ = f32[12,128]{1,0:T(8,128)S(1)} collective-permute-done((f32[12,128]{1,0:T(8,128)S(1)}, f32[12,128]{1,0:T(8,128)S(1)}, u32[]{:S(2)}, u32[]{:S(2)}) %collective-permute-start.7) | collective-permute-done | bytes 6176 | tf_op jit(solution)/shard_map/ppermute | solution.py:52
  25.6 1.8 %shard_map.112 = (f32[16,128]{1,0:T(8,128)S(1)}, f32[8,128]{1,0:T(8,128)S(1)}, f32[8,128]{1,0:T(8,128)S(1)}, f32[8,128]{1,0:T(8,128)S(1)}, f32[8,128]{1,0:T(8,128)S(1)}) custom-call(f32[6,80,128]{2,1,0:T(8,128)S(1)} %shard_map.111.refs_0_, s32[80,128]{1,0:T(8,128)S(1)} %get-tuple-element.53.nodes_ref.refs_1_, ...), custom_call_target="tpu_custom_call" | custom-call | tf_op jit(solution)/shard_map/pallas_call | solution.py:580
  27.4 0.7 %collective-permute-start.10 = (f32[8,128]{1,0:T(8,128)S(1)}, f32[8,128]{1,0:T(8,128)S(1)}, u32[]{:S(2)}, u32[]{:S(2)}) collective-permute-start(f32[8,128]{1,0:T(8,128)S(1)} %get-tuple-element.65), channel_id=1, source_target_pairs={{4,8},{8,4},{12,16},{16,12},{20,24},{24,20},{5,9},{9,5},{13,17},{1... | collective-permute-start | bytes 12296 | tf_op jit(solution)/shard_map/ppermute | solution.py:52
  28.0 5.2 %collective-permute-start.9 = (f32[8,128]{1,0:T(8,128)S(1)}, f32[8,128]{1,0:T(8,128)S(1)}, u32[]{:S(2)}, u32[]{:S(2)}) collective-permute-start(f32[8,128]{1,0:T(8,128)S(1)} %get-tuple-element.64), channel_id=1, source_target_pairs={{0,4},{4,0},{8,12},{12,8},{16,20},{20,16},{24,28},{28,24},{1,5},{5... | collective-permute-start | bytes 12296 | tf_op jit(solution)/shard_map/ppermute | solution.py:52
  33.3 1.5 %collective-permute-start.11 = (f32[8,128]{1,0:T(8,128)S(1)}, f32[8,128]{1,0:T(8,128)S(1)}, u32[]{:S(2)}, u32[]{:S(2)}) collective-permute-start(f32[8,128]{1,0:T(8,128)S(1)} %get-tuple-element.68), channel_id=1, source_target_pairs={{0,2},{2,0},{1,3},{3,1},{4,6},{6,4},{5,7},{7,5},{8,10},{10,8},{9,1... | collective-permute-start | bytes 12296 | tf_op jit(solution)/shard_map/ppermute | solution.py:52
  34.8 0.1 collective-permute-done.9.refs_0_
  34.9 0.6 %shard_map.113 = (f32[16,128]{1,0:T(8,128)S(1)}, f32[24,128]{1,0:T(8,128)}) custom-call(f32[16,128]{1,0:T(8,128)S(1)} %get-tuple-element.61.own_ref, s32[12,128]{1,0:T(8,128)S(1)} %get-tuple-element.51.halos_ref, bf16[1536,128]{1,0:T(8,128)(2,1)S(1)} %get-tuple-element.62.halo_hot_ref, f32[24,128]{1,0:T(8,128)S(1)} %get-tuple-element.63.state_in_ref, ...), custom_call_target="tpu_custom_call" | custom-call | tf_op jit(solution)/shard_map/pallas_call | solution.py:595
  35.5 1.4 %collective-permute-done.11.refs_0_ = f32[8,128]{1,0:T(8,128)S(1)} collective-permute-done((f32[8,128]{1,0:T(8,128)S(1)}, f32[8,128]{1,0:T(8,128)S(1)}, u32[]{:S(2)}, u32[]{:S(2)}) %collective-permute-start.11) | collective-permute-done | bytes 4128 | tf_op jit(solution)/shard_map/ppermute | solution.py:52
  36.9 0.8 %shard_map.114 = f32[4,512]{1,0:T(4,128)} custom-call(f32[16,128]{1,0:T(8,128)S(1)} %get-tuple-element.67.sums_ref, s32[12,128]{1,0:T(8,128)S(1)} %get-tuple-element.51.halos_ref, bf16[1536,128]{1,0:T(8,128)(2,1)S(1)} %get-tuple-element.62.halo_hot_ref, f32[8,128]{1,0:T(8,128)S(1)} %collective-permute-done.11.refs_0_, ...), custom_call_target="tpu_custom_call" | custom-call | tf_op jit(solution)/shard_map/pallas_call | solution.py:602
  (9 shorter events, 0.1 us)
Async XLA Ops:
  1.9 1.5 %collective-permute-start.2 = (f32[192,128]{1,0:T(8,128)S(1)}, f32[192,128]{1,0:T(8,128)S(1)}, u32[]{:S(2)}, u32[]{:S(2)}) collective-permute-start(f32[192,128]{1,0:T(8,128)S(1)} %get-tuple-element.47), channel_id=1, source_target_pairs={{0,1},{1,0},{2,3},{3,2},{4,5},{5,4},{6,7},{7,6},{8,9},{9,8},{10,11... | collective-permute-start | bytes 294920 | tf_op jit(solution)/shard_map/ppermute | solution.py:509
  2.4 5.9 %collective-permute-start = (f32[224,128]{1,0:T(8,128)S(1)}, f32[224,128]{1,0:T(8,128)S(1)}, u32[]{:S(2)}, u32[]{:S(2)}) collective-permute-start(f32[224,128]{1,0:T(8,128)S(1)} %get-tuple-element.39), channel_id=1, source_target_pairs={{0,1},{1,0},{2,3},{3,2},{4,5},{5,4},{6,7},{7,6},{8,9},{9,8},{10,11... | collective-permute-start | bytes 344072 | tf_op jit(solution)/shard_map/ppermute | solution.py:510
  3.4 11.1 %collective-permute-start.3 = (f32[384,128]{1,0:T(8,128)S(1)}, f32[384,128]{1,0:T(8,128)S(1)}, u32[]{:S(2)}, u32[]{:S(2)}) collective-permute-start(f32[384,128]{1,0:T(8,128)S(1)} %pad_maximum_fusion.1), channel_id=1, source_target_pairs={{5,9},{9,5},{13,17},{17,13},{21,25},{25,21},{0,8},{8,0},{4,12},{12... | collective-permute-start | bytes 589832 | tf_op jit(solution)/shard_map/ppermute | solution.py:513
  8.3 7.6 %collective-permute-start.1 = (f32[384,128]{1,0:T(8,128)S(1)}, f32[384,128]{1,0:T(8,128)S(1)}, u32[]{:S(2)}, u32[]{:S(2)}) collective-permute-start(f32[384,128]{1,0:T(8,128)S(1)} %pad_maximum_fusion), channel_id=1, source_target_pairs={{0,4},{4,0},{8,12},{12,8},{16,20},{20,16},{24,28},{28,24},{9,17},{... | collective-permute-start | bytes 589832 | tf_op jit(solution)/shard_map/ppermute | solution.py:513
  16.4 1.2 %collective-permute-start.4 = (f32[24,128]{1,0:T(8,128)S(1)}, f32[24,128]{1,0:T(8,128)S(1)}, u32[]{:S(2)}, u32[]{:S(2)}) collective-permute-start(f32[24,128]{1,0:T(8,128)S(1)} %shard_map.109), channel_id=1, source_target_pairs={{0,1},{1,0},{2,3},{3,2},{4,5},{5,4},{6,7},{7,6},{8,9},{9,8},{10,11... | collective-permute-start | bytes 36872 | tf_op jit(solution)/shard_map/ppermute | solution.py:557
  17.8 5.9 %collective-permute-start.5 = (f32[12,128]{1,0:T(8,128)S(1)}, f32[12,128]{1,0:T(8,128)S(1)}, u32[]{:S(2)}, u32[]{:S(2)}) collective-permute-start(f32[12,128]{1,0:T(8,128)S(1)} %get-tuple-element.54), channel_id=1, source_target_pairs={{4,8},{8,4},{12,16},{16,12},{20,24},{24,20},{5,9},{9,5},{13,17},{1... | collective-permute-start | bytes 18440 | tf_op jit(solution)/shard_map/ppermute | solution.py:52
  18.4 5.2 %collective-permute-start.6 = (f32[12,128]{1,0:T(8,128)S(1)}, f32[12,128]{1,0:T(8,128)S(1)}, u32[]{:S(2)}, u32[]{:S(2)}) collective-permute-start(f32[12,128]{1,0:T(8,128)S(1)} %get-tuple-element.55), channel_id=1, source_target_pairs={{0,4},{4,0},{8,12},{12,8},{16,20},{20,16},{24,28},{28,24},{1,5},{5... | collective-permute-start | bytes 18440 | tf_op jit(solution)/shard_map/ppermute | solution.py:52
  21.9 3.7 %collective-permute-start.7 = (f32[12,128]{1,0:T(8,128)S(1)}, f32[12,128]{1,0:T(8,128)S(1)}, u32[]{:S(2)}, u32[]{:S(2)}) collective-permute-start(f32[12,128]{1,0:T(8,128)S(1)} %get-tuple-element.59), channel_id=1, source_target_pairs={{0,2},{2,0},{1,3},{3,1},{4,6},{6,4},{5,7},{7,5},{8,10},{10,8},{9,1... | collective-permute-start | bytes 18440 | tf_op jit(solution)/shard_map/ppermute | solution.py:52
  23.6 1.9 %collective-permute-start.8 = (f32[12,128]{1,0:T(8,128)S(1)}, f32[12,128]{1,0:T(8,128)S(1)}, u32[]{:S(2)}, u32[]{:S(2)}) collective-permute-start(f32[12,128]{1,0:T(8,128)S(1)} %get-tuple-element.60), channel_id=1, source_target_pairs={{0,1},{1,0},{2,3},{3,2},{4,5},{5,4},{6,7},{7,6},{8,9},{9,8},{10,11... | collective-permute-start | bytes 18440 | tf_op jit(solution)/shard_map/ppermute | solution.py:52
  27.4 7.4 %collective-permute-start.10 = (f32[8,128]{1,0:T(8,128)S(1)}, f32[8,128]{1,0:T(8,128)S(1)}, u32[]{:S(2)}, u32[]{:S(2)}) collective-permute-start(f32[8,128]{1,0:T(8,128)S(1)} %get-tuple-element.65), channel_id=1, source_target_pairs={{4,8},{8,4},{12,16},{16,12},{20,24},{24,20},{5,9},{9,5},{13,17},{1... | collective-permute-start | bytes 12296 | tf_op jit(solution)/shard_map/ppermute | solution.py:52
  28.0 6.8 %collective-permute-start.9 = (f32[8,128]{1,0:T(8,128)S(1)}, f32[8,128]{1,0:T(8,128)S(1)}, u32[]{:S(2)}, u32[]{:S(2)}) collective-permute-start(f32[8,128]{1,0:T(8,128)S(1)} %get-tuple-element.64), channel_id=1, source_target_pairs={{0,4},{4,0},{8,12},{12,8},{16,20},{20,16},{24,28},{28,24},{1,5},{5... | collective-permute-start | bytes 12296 | tf_op jit(solution)/shard_map/ppermute | solution.py:52
  33.3 3.6 %collective-permute-start.11 = (f32[8,128]{1,0:T(8,128)S(1)}, f32[8,128]{1,0:T(8,128)S(1)}, u32[]{:S(2)}, u32[]{:S(2)}) collective-permute-start(f32[8,128]{1,0:T(8,128)S(1)} %get-tuple-element.68), channel_id=1, source_target_pairs={{0,2},{2,0},{1,3},{3,1},{4,6},{6,4},{5,7},{7,5},{8,10},{10,8},{9,1... | collective-permute-start | bytes 12296 | tf_op jit(solution)/shard_map/ppermute | solution.py:52
  34.8 2.1 %collective-permute-start.12 = (f32[8,128]{1,0:T(8,128)S(1)}, f32[8,128]{1,0:T(8,128)S(1)}, u32[]{:S(2)}, u32[]{:S(2)}) collective-permute-start(f32[8,128]{1,0:T(8,128)S(1)} %get-tuple-element.69), channel_id=1, source_target_pairs={{0,1},{1,0},{2,3},{3,2},{4,5},{5,4},{6,7},{7,6},{8,9},{9,8},{10,11... | collective-permute-start | bytes 12296 | tf_op jit(solution)/shard_map/ppermute | solution.py:52

commit v3 on v2

--- a/solution.py
+++ b/solution.py
@@ -60,7 +60,7 @@
 
 def pack_blocks(blocks_ref, old_ref, ref, offset):
     slots = blocks_ref.shape[2]
-    stride = old_ref.shape[0] // FIELDS
+    stride = old_ref.shape[0] // (FIELDS + 1)
     for to_layer in range(2):
         peer = (offset + REACH) * 2 + to_layer
         start = to_layer * FIELDS * slots
@@ -75,7 +75,7 @@
     held = refs[5 + count : 5 + 2 * count]
     blocks_ref, sems = refs[5 + 2 * count :]
     first = [pltpu.make_async_copy(blocks_in_ref, blocks_ref, sems.at[0])]
-    first += [pltpu.make_async_copy(old_in_ref, old_ref, sems.at[1])]
+    first += [pltpu.make_async_copy(old_in_ref, old_ref.at[: old_in_ref.shape[0]], sems.at[1])]
     rest = [pltpu.make_async_copy(refs[2 + i], held[i], sems.at[2 + i]) for i in range(count)]
     for copy in first + rest:
         copy.start()
@@ -185,7 +185,7 @@
     for layer in range(2):
         chunk_ref = own_ref.at[layer]
         for c in range(blocks_ref.shape[2]):
-            rows = pl.ds(blocks_ref[2 * REACH + layer, 0, c], FIELDS, stride=old_ref.shape[0] // FIELDS)
+            rows = pl.ds(blocks_ref[2 * REACH + layer, 0, c], FIELDS, stride=old_ref.shape[0] // (FIELDS + 1))
             chunk_ref[FIELDS * c : FIELDS * (c + 1), :] = old_ref[rows, :]
     for k in range(halos_in_ref.shape[0]):
         cut_rows(halos_in_ref.at[k], halos_ref.at[2 * k : 2 * k + 2])
@@ -490,7 +490,7 @@
     give_rows = 2 * rows + 2 * slot_rows
     give_first, give, old_rows, *held = pl.pallas_call(
         functools.partial(give_kernel, count),
-        out_shape=[shaped(2 * rows, BLOCK), shaped(give_rows, BLOCK), shaped(*old_rows.shape)]
+        out_shape=[shaped(2 * rows, BLOCK), shaped(give_rows, BLOCK), shaped(old_rows.shape[0] // FIELDS * (FIELDS + 1), BLOCK)]
         + [jax.ShapeDtypeStruct(a.shape, a.dtype) for a in arguments],
         in_specs=[pl.BlockSpec(memory_space=pltpu.HBM)] * (2 + count),
         out_specs=[VMEM] * (3 + count),

time: 37.9 us -> 37.9 us (level)
  no operation moved by 1% of the time
where the time goes in v3:
time: 37.9 us; the launch traced here: 37.7 us
  starting transfers between devices  22.3 us (59%)
  Pallas kernels  10.6 us (28%)
  waiting for transfers between devices  4 us (11%)
  between operations  0.78 us (2%)
    ppermute x8, starting transfers between devices, pair_swap(): lax.ppermute(value, axis, both_ways([(at, at + 1) for at in range(first,...  13.3 us
    ppermute x2, starting transfers between devices, per_device(): lax.ppermute(part, ('mapx', 'layer'), pairs).reshape(4, rows, BLOCK)  8.31 us
    ppermute x8, waiting for transfers between devices, pair_swap(): lax.ppermute(value, axis, both_ways([(at, at + 1) for at in range(first,...  2.76 us
    pallas_call x1, Pallas kernels, per_device(): pl.pallas_call(own_kernel, out_shape=(shaped(2, FIELDS, slot_rows, BLOCK)...  2.69 us
    pallas_call x1, Pallas kernels, per_device(): pl.pallas_call(functools.partial(element_kernel, sizes, moves, owned_slot...  1.81 us
    pallas_call x1, Pallas kernels, per_device(): pl.pallas_call(functools.partial(give_kernel, count), out_shape=[shaped(2...  1.26 us
    pallas_call x2, Pallas kernels, per_device(): pl.pallas_call(functools.partial(late_kernel, owned // BLOCK, owner), out...  0.96 us
    pallas_call x1, Pallas kernels, per_device(): pl.pallas_call(early_kernel, out_shape=shaped(2, FIELDS, slot_rows, BLOCK...  0.89 us
  transfers between devices with their start and end apart: 13, of which 5 were waited for; matrix products, arithmetic and copies ran while one was open for 0% of the time, Pallas kernels for 16%

profile of v3, /device:TPU:0, one launch (start us, length us, event | category | flops | bytes accessed | tf_op | source)
XLA Modules:
  0.0 37.7 jit_solution(2320094616239193813)
XLA Ops:
  0.6 1.3 %shard_map.104 = (f32[192,128]{1,0:T(8,128)S(1)}, f32[224,128]{1,0:T(8,128)S(1)}, f32[448,128]{1,0:T(8,128)S(1)}, s32[4,512]{1,0:T(4,128)S(1)}, f32[4,512]{1,0:T...) custom-call(s32[10,1,16]{2,1,0:T(1,128)} %bitcast.19, ...), custom_call_target="tpu_custom_call" | custom-call | tf_op jit(solution)/shard_map/pallas_call | solution.py:491
  1.9 0.5 %collective-permute-start.2 = (f32[192,128]{1,0:T(8,128)S(1)}, f32[192,128]{1,0:T(8,128)S(1)}, u32[]{:S(2)}, u32[]{:S(2)}) collective-permute-start(f32[192,128]{1,0:T(8,128)S(1)} %get-tuple-element.47), channel_id=1, source_target_pairs={{0,1},{1,0},{2,3},{3,2},{4,5},{5,4},{6,7},{7,6},{8,9},{9,8},{10,11... | collective-permute-start | bytes 294920 | tf_op jit(solution)/shard_map/ppermute | solution.py:509
  2.4 0.1 collective-permute-start
  2.5 0.8 %shard_map.105 = (f32[192,128]{1,0:T(8,128)S(1)}, f32[192,128]{1,0:T(8,128)S(1)}) custom-call(s32[10,1,16]{2,1,0:T(1,128)S(1)} %get-tuple-element.36.blocks_ref, f32[448,128]{1,0:T(8,128)S(1)} %get-tuple-element.37.old_ref), custom_call_target="tpu_custom_call" | custom-call | tf_op jit(solution)/shard_map/pallas_call | solution.py:501
  3.3 0.0 collective-permute-done.2
  3.4 4.9 %collective-permute-start.3 = (f32[384,128]{1,0:T(8,128)S(1)}, f32[384,128]{1,0:T(8,128)S(1)}, u32[]{:S(2)}, u32[]{:S(2)}) collective-permute-start(f32[384,128]{1,0:T(8,128)S(1)} %pad_maximum_fusion.1), channel_id=1, source_target_pairs={{5,9},{9,5},{13,17},{17,13},{21,25},{25,21},{0,8},{8,0},{4,12},{12... | collective-permute-start | bytes 589832 | tf_op jit(solution)/shard_map/ppermute | solution.py:513
  8.3 3.4 %collective-permute-start.1 = (f32[384,128]{1,0:T(8,128)S(1)}, f32[384,128]{1,0:T(8,128)S(1)}, u32[]{:S(2)}, u32[]{:S(2)}) collective-permute-start(f32[384,128]{1,0:T(8,128)S(1)} %pad_maximum_fusion), channel_id=1, source_target_pairs={{0,4},{4,0},{8,12},{12,8},{16,20},{20,16},{24,28},{28,24},{9,17},{... | collective-permute-start | bytes 589832 | tf_op jit(solution)/shard_map/ppermute | solution.py:513
  11.8 2.7 %shard_map.106 = (f32[2,6,16,128]{3,2,1,0:T(8,128)S(1)}, s32[2,16,128]{2,1,0:T(8,128)S(1)}, f32[16,128]{1,0:T(8,128)S(1)}, s32[12,128]{1,0:T(8,128)S(1)}, s32[80...) custom-call(s32[10,1,16]{2,1,0:T(1,128)S(1)} %get-tuple-element.36.b, ...), custom_call_target="tpu_custom_call" | custom-call | tf_op jit(solution)/shard_map/pallas_call | solution.py:522
  14.5 0.0 collective-permute-done.3
  14.5 0.9 %shard_map.107.found_ref = f32[2,6,16,128]{3,2,1,0:T(8,128)S(1)} custom-call(f32[4,96,128]{2,1,0:T(8,128)S(1)} %bitcast.15, s32[2,16,128]{2,1,0:T(8,128)S(1)} %get-tuple-element.45.slots_ref, f32[2,6,16,128]{3,2,1,0:T(8,128)S(1)} %get-tuple-element.48.found_in_ref), custom_call_target="tpu_custom_call" | custom-call | tf_op jit(solution)/shard_map/pallas_call | solution.py:539
  15.4 0.5 %collective-permute-done.1 = f32[384,128]{1,0:T(8,128)S(1)} collective-permute-done((f32[384,128]{1,0:T(8,128)S(1)}, f32[384,128]{1,0:T(8,128)S(1)}, u32[]{:S(2)}, u32[]{:S(2)}) %collective-permute-start.1) | collective-permute-done | bytes 196640 | tf_op jit(solution)/shard_map/ppermute | solution.py:513
  15.9 0.5 %shard_map.109 = f32[24,128]{1,0:T(8,128)S(1)} custom-call(f32[4,96,128]{2,1,0:T(8,128)S(1)} %bitcast.13, s32[2,16,128]{2,1,0:T(8,128)S(1)} %get-tuple-element.45.slots_ref, f32[2,6,16,128]{3,2,1,0:T(8,128)S(1)} %shard_map.107.found_ref, f32[16,128]{1,0:T(8,128)S(1)} %get-tuple-element.74.weights_ref), custom_call_target="tpu_custom_call" | custom-call | tf_op jit(solution)/shard_map/pallas_call | solution.py:548
  16.4 0.1 collective-permute-start.4
  16.5 0.5 %shard_map.108.mine_ref = f32[24,128]{1,0:T(8,128)S(1)} custom-call(f32[4,96,128]{2,1,0:T(8,128)S(1)} %bitcast.14, s32[2,16,128]{2,1,0:T(8,128)S(1)} %get-tuple-element.45.slots_ref, f32[2,6,16,128]{3,2,1,0:T(8,128)S(1)} %shard_map.107.found_ref, f32[16,128]{1,0:T(8,128)S(1)} %get-tuple-element.49.weights_ref), custom_call_target="tpu_custom_call" | custom-call | tf_op jit(solution)/shard_map/pallas_call | solution.py:548
  17.0 0.7 %collective-permute-done.4.came_ref = f32[24,128]{1,0:T(8,128)S(1)} collective-permute-done((f32[24,128]{1,0:T(8,128)S(1)}, f32[24,128]{1,0:T(8,128)S(1)}, u32[]{:S(2)}, u32[]{:S(2)}) %collective-permute-start.4) | collective-permute-done | bytes 12320 | tf_op jit(solution)/shard_map/ppermute | solution.py:557
  17.6 0.1 shard_map.110
  17.8 0.7 %collective-permute-start.5 = (f32[12,128]{1,0:T(8,128)S(1)}, f32[12,128]{1,0:T(8,128)S(1)}, u32[]{:S(2)}, u32[]{:S(2)}) collective-permute-start(f32[12,128]{1,0:T(8,128)S(1)} %get-tuple-element.54), channel_id=1, source_target_pairs={{4,8},{8,4},{12,16},{16,12},{20,24},{24,20},{5,9},{9,5},{13,17},{1... | collective-permute-start | bytes 18440 | tf_op jit(solution)/shard_map/ppermute | solution.py:52
  18.4 3.5 %collective-permute-start.6 = (f32[12,128]{1,0:T(8,128)S(1)}, f32[12,128]{1,0:T(8,128)S(1)}, u32[]{:S(2)}, u32[]{:S(2)}) collective-permute-start(f32[12,128]{1,0:T(8,128)S(1)} %get-tuple-element.55), channel_id=1, source_target_pairs={{0,4},{4,0},{8,12},{12,8},{16,20},{20,16},{24,28},{28,24},{1,5},{5... | collective-permute-start | bytes 18440 | tf_op jit(solution)/shard_map/ppermute | solution.py:52
  21.9 1.7 %collective-permute-start.7 = (f32[12,128]{1,0:T(8,128)S(1)}, f32[12,128]{1,0:T(8,128)S(1)}, u32[]{:S(2)}, u32[]{:S(2)}) collective-permute-start(f32[12,128]{1,0:T(8,128)S(1)} %get-tuple-element.59), channel_id=1, source_target_pairs={{0,2},{2,0},{1,3},{3,1},{4,6},{6,4},{5,7},{7,5},{8,10},{10,8},{9,1... | collective-permute-start | bytes 18440 | tf_op jit(solution)/shard_map/ppermute | solution.py:52
  23.6 0.0 collective-permute-start.8
  23.7 0.6 %shard_map.111.refs_0_ = f32[6,80,128]{2,1,0:T(8,128)S(1)} custom-call(f32[2,12,128]{2,1,0:T(8,128)S(1)} %get-tuple-element.52.table_ref, s32[80,128]{1,0:T(8,128)S(1)} %get-tuple-element.53.nodes_ref.refs_1_, f32[12,128]{1,0:T(8,128)S(1)} %collective-permute-done.5.refs_0_, f32[12,128]{1,0:T(8,128)S(1)} %collective-permute-done.6.refs_1_), custom_call_target="tpu_custom_call" | custom-call | tf_op jit(solution)/shard_map/pallas_call | solution.py:573
  24.3 1.3 %collective-permute-done.7.refs_5_ = f32[12,128]{1,0:T(8,128)S(1)} collective-permute-done((f32[12,128]{1,0:T(8,128)S(1)}, f32[12,128]{1,0:T(8,128)S(1)}, u32[]{:S(2)}, u32[]{:S(2)}) %collective-permute-start.7) | collective-permute-done | bytes 6176 | tf_op jit(solution)/shard_map/ppermute | solution.py:52
  25.6 0.0 collective-permute-done.8.refs_6_
  25.6 1.8 %shard_map.112 = (f32[16,128]{1,0:T(8,128)S(1)}, f32[8,128]{1,0:T(8,128)S(1)}, f32[8,128]{1,0:T(8,128)S(1)}, f32[8,128]{1,0:T(8,128)S(1)}, f32[8,128]{1,0:T(8,128)S(1)}) custom-call(f32[6,80,128]{2,1,0:T(8,128)S(1)} %shard_map.111.refs_0_, s32[80,128]{1,0:T(8,128)S(1)} %get-tuple-element.53.nodes_ref.refs_1_, ...), custom_call_target="tpu_custom_call" | custom-call | tf_op jit(solution)/shard_map/pallas_call | solution.py:580
  27.4 0.7 %collective-permute-start.10 = (f32[8,128]{1,0:T(8,128)S(1)}, f32[8,128]{1,0:T(8,128)S(1)}, u32[]{:S(2)}, u32[]{:S(2)}) collective-permute-start(f32[8,128]{1,0:T(8,128)S(1)} %get-tuple-element.65), channel_id=1, source_target_pairs={{4,8},{8,4},{12,16},{16,12},{20,24},{24,20},{5,9},{9,5},{13,17},{1... | collective-permute-start | bytes 12296 | tf_op jit(solution)/shard_map/ppermute | solution.py:52
  28.0 5.2 %collective-permute-start.9 = (f32[8,128]{1,0:T(8,128)S(1)}, f32[8,128]{1,0:T(8,128)S(1)}, u32[]{:S(2)}, u32[]{:S(2)}) collective-permute-start(f32[8,128]{1,0:T(8,128)S(1)} %get-tuple-element.64), channel_id=1, source_target_pairs={{0,4},{4,0},{8,12},{12,8},{16,20},{20,16},{24,28},{28,24},{1,5},{5... | collective-permute-start | bytes 12296 | tf_op jit(solution)/shard_map/ppermute | solution.py:52
  33.3 1.5 %collective-permute-start.11 = (f32[8,128]{1,0:T(8,128)S(1)}, f32[8,128]{1,0:T(8,128)S(1)}, u32[]{:S(2)}, u32[]{:S(2)}) collective-permute-start(f32[8,128]{1,0:T(8,128)S(1)} %get-tuple-element.68), channel_id=1, source_target_pairs={{0,2},{2,0},{1,3},{3,1},{4,6},{6,4},{5,7},{7,5},{8,10},{10,8},{9,1... | collective-permute-start | bytes 12296 | tf_op jit(solution)/shard_map/ppermute | solution.py:52
  34.8 0.0 collective-permute-start.12
  34.8 0.1 collective-permute-done.9.refs_0_
  34.9 0.6 %shard_map.113 = (f32[16,128]{1,0:T(8,128)S(1)}, f32[24,128]{1,0:T(8,128)}) custom-call(f32[16,128]{1,0:T(8,128)S(1)} %get-tuple-element.61.own_ref, s32[12,128]{1,0:T(8,128)S(1)} %get-tuple-element.51.halos_ref, bf16[1536,128]{1,0:T(8,128)(2,1)S(1)} %get-tuple-element.62.halo_hot_ref, f32[24,128]{1,0:T(8,128)S(1)} %get-tuple-element.63.state_in_ref, ...), custom_call_target="tpu_custom_call" | custom-call | tf_op jit(solution)/shard_map/pallas_call | solution.py:595
  35.5 1.4 %collective-permute-done.11.refs_0_ = f32[8,128]{1,0:T(8,128)S(1)} collective-permute-done((f32[8,128]{1,0:T(8,128)S(1)}, f32[8,128]{1,0:T(8,128)S(1)}, u32[]{:S(2)}, u32[]{:S(2)}) %collective-permute-start.11) | collective-permute-done | bytes 4128 | tf_op jit(solution)/shard_map/ppermute | solution.py:52
  36.9 0.8 %shard_map.114 = f32[4,512]{1,0:T(4,128)} custom-call(f32[16,128]{1,0:T(8,128)S(1)} %get-tuple-element.67.sums_ref, s32[12,128]{1,0:T(8,128)S(1)} %get-tuple-element.51.halos_ref, bf16[1536,128]{1,0:T(8,128)(2,1)S(1)} %get-tuple-element.62.halo_hot_ref, f32[8,128]{1,0:T(8,128)S(1)} %collective-permute-done.11.refs_0_, ...), custom_call_target="tpu_custom_call" | custom-call | tf_op jit(solution)/shard_map/pallas_call | solution.py:602
  (9 shorter events, 0.1 us)
Async XLA Ops:
  1.9 1.5 %collective-permute-start.2 = (f32[192,128]{1,0:T(8,128)S(1)}, f32[192,128]{1,0:T(8,128)S(1)}, u32[]{:S(2)}, u32[]{:S(2)}) collective-permute-start(f32[192,128]{1,0:T(8,128)S(1)} %get-tuple-element.47), channel_id=1, source_target_pairs={{0,1},{1,0},{2,3},{3,2},{4,5},{5,4},{6,7},{7,6},{8,9},{9,8},{10,11... | collective-permute-start | bytes 294920 | tf_op jit(solution)/shard_map/ppermute | solution.py:509
  2.4 5.9 %collective-permute-start = (f32[224,128]{1,0:T(8,128)S(1)}, f32[224,128]{1,0:T(8,128)S(1)}, u32[]{:S(2)}, u32[]{:S(2)}) collective-permute-start(f32[224,128]{1,0:T(8,128)S(1)} %get-tuple-element.39), channel_id=1, source_target_pairs={{0,1},{1,0},{2,3},{3,2},{4,5},{5,4},{6,7},{7,6},{8,9},{9,8},{10,11... | collective-permute-start | bytes 344072 | tf_op jit(solution)/shard_map/ppermute | solution.py:510
  3.4 11.1 %collective-permute-start.3 = (f32[384,128]{1,0:T(8,128)S(1)}, f32[384,128]{1,0:T(8,128)S(1)}, u32[]{:S(2)}, u32[]{:S(2)}) collective-permute-start(f32[384,128]{1,0:T(8,128)S(1)} %pad_maximum_fusion.1), channel_id=1, source_target_pairs={{5,9},{9,5},{13,17},{17,13},{21,25},{25,21},{0,8},{8,0},{4,12},{12... | collective-permute-start | bytes 589832 | tf_op jit(solution)/shard_map/ppermute | solution.py:513
  8.3 7.6 %collective-permute-start.1 = (f32[384,128]{1,0:T(8,128)S(1)}, f32[384,128]{1,0:T(8,128)S(1)}, u32[]{:S(2)}, u32[]{:S(2)}) collective-permute-start(f32[384,128]{1,0:T(8,128)S(1)} %pad_maximum_fusion), channel_id=1, source_target_pairs={{0,4},{4,0},{8,12},{12,8},{16,20},{20,16},{24,28},{28,24},{9,17},{... | collective-permute-start | bytes 589832 | tf_op jit(solution)/shard_map/ppermute | solution.py:513
  16.4 1.2 %collective-permute-start.4 = (f32[24,128]{1,0:T(8,128)S(1)}, f32[24,128]{1,0:T(8,128)S(1)}, u32[]{:S(2)}, u32[]{:S(2)}) collective-permute-start(f32[24,128]{1,0:T(8,128)S(1)} %shard_map.109), channel_id=1, source_target_pairs={{0,1},{1,0},{2,3},{3,2},{4,5},{5,4},{6,7},{7,6},{8,9},{9,8},{10,11... | collective-permute-start | bytes 36872 | tf_op jit(solution)/shard_map/ppermute | solution.py:557
  17.8 5.9 %collective-permute-start.5 = (f32[12,128]{1,0:T(8,128)S(1)}, f32[12,128]{1,0:T(8,128)S(1)}, u32[]{:S(2)}, u32[]{:S(2)}) collective-permute-start(f32[12,128]{1,0:T(8,128)S(1)} %get-tuple-element.54), channel_id=1, source_target_pairs={{4,8},{8,4},{12,16},{16,12},{20,24},{24,20},{5,9},{9,5},{13,17},{1... | collective-permute-start | bytes 18440 | tf_op jit(solution)/shard_map/ppermute | solution.py:52
  18.4 5.2 %collective-permute-start.6 = (f32[12,128]{1,0:T(8,128)S(1)}, f32[12,128]{1,0:T(8,128)S(1)}, u32[]{:S(2)}, u32[]{:S(2)}) collective-permute-start(f32[12,128]{1,0:T(8,128)S(1)} %get-tuple-element.55), channel_id=1, source_target_pairs={{0,4},{4,0},{8,12},{12,8},{16,20},{20,16},{24,28},{28,24},{1,5},{5... | collective-permute-start | bytes 18440 | tf_op jit(solution)/shard_map/ppermute | solution.py:52
  21.9 3.7 %collective-permute-start.7 = (f32[12,128]{1,0:T(8,128)S(1)}, f32[12,128]{1,0:T(8,128)S(1)}, u32[]{:S(2)}, u32[]{:S(2)}) collective-permute-start(f32[12,128]{1,0:T(8,128)S(1)} %get-tuple-element.59), channel_id=1, source_target_pairs={{0,2},{2,0},{1,3},{3,1},{4,6},{6,4},{5,7},{7,5},{8,10},{10,8},{9,1... | collective-permute-start | bytes 18440 | tf_op jit(solution)/shard_map/ppermute | solution.py:52
  23.6 1.9 %collective-permute-start.8 = (f32[12,128]{1,0:T(8,128)S(1)}, f32[12,128]{1,0:T(8,128)S(1)}, u32[]{:S(2)}, u32[]{:S(2)}) collective-permute-start(f32[12,128]{1,0:T(8,128)S(1)} %get-tuple-element.60), channel_id=1, source_target_pairs={{0,1},{1,0},{2,3},{3,2},{4,5},{5,4},{6,7},{7,6},{8,9},{9,8},{10,11... | collective-permute-start | bytes 18440 | tf_op jit(solution)/shard_map/ppermute | solution.py:52
  27.4 7.4 %collective-permute-start.10 = (f32[8,128]{1,0:T(8,128)S(1)}, f32[8,128]{1,0:T(8,128)S(1)}, u32[]{:S(2)}, u32[]{:S(2)}) collective-permute-start(f32[8,128]{1,0:T(8,128)S(1)} %get-tuple-element.65), channel_id=1, source_target_pairs={{4,8},{8,4},{12,16},{16,12},{20,24},{24,20},{5,9},{9,5},{13,17},{1... | collective-permute-start | bytes 12296 | tf_op jit(solution)/shard_map/ppermute | solution.py:52
  28.0 6.8 %collective-permute-start.9 = (f32[8,128]{1,0:T(8,128)S(1)}, f32[8,128]{1,0:T(8,128)S(1)}, u32[]{:S(2)}, u32[]{:S(2)}) collective-permute-start(f32[8,128]{1,0:T(8,128)S(1)} %get-tuple-element.64), channel_id=1, source_target_pairs={{0,4},{4,0},{8,12},{12,8},{16,20},{20,16},{24,28},{28,24},{1,5},{5... | collective-permute-start | bytes 12296 | tf_op jit(solution)/shard_map/ppermute | solution.py:52
  33.3 3.6 %collective-permute-start.11 = (f32[8,128]{1,0:T(8,128)S(1)}, f32[8,128]{1,0:T(8,128)S(1)}, u32[]{:S(2)}, u32[]{:S(2)}) collective-permute-start(f32[8,128]{1,0:T(8,128)S(1)} %get-tuple-element.68), channel_id=1, source_target_pairs={{0,2},{2,0},{1,3},{3,1},{4,6},{6,4},{5,7},{7,5},{8,10},{10,8},{9,1... | collective-permute-start | bytes 12296 | tf_op jit(solution)/shard_map/ppermute | solution.py:52
  34.8 2.1 %collective-permute-start.12 = (f32[8,128]{1,0:T(8,128)S(1)}, f32[8,128]{1,0:T(8,128)S(1)}, u32[]{:S(2)}, u32[]{:S(2)}) collective-permute-start(f32[8,128]{1,0:T(8,128)S(1)} %get-tuple-element.69), channel_id=1, source_target_pairs={{0,1},{1,0},{2,3},{3,2},{4,5},{5,4},{6,7},{7,6},{8,9},{9,8},{10,11... | collective-permute-start | bytes 12296 | tf_op jit(solution)/shard_map/ppermute | solution.py:52
